TPU v7x, 256 devices: a whole 4x4x8 slice. The times are simulated.
256 devices in a mesh: term: 8 (over x, core), sector: 32 (over y, z).
Axes of the slice: x: 4, y: 4, z: 8, core: 2. Of those that a mesh axis runs over, the one named last changes fastest.
Arguments:
- psi: bfloat16 [256, 256, 256], P('sector'), may hold values from -6 to 6
- left_env: bfloat16 [8, 128, 4, 256, 256], P('term', 'sector'), may hold values from -0.375 to 0.375
- right_env: bfloat16 [8, 128, 4, 256, 256], P('term', 'sector'), may hold values from -0.375 to 0.375
- pair_source: int32 [1024], P('sector'), may hold values from 0 to 7
- pair_left: int32 [1024], P('sector'), may hold values from 0 to 3
- pair_right: int32 [1024], P('sector'), may hold values from 0 to 3
- pair_dest: int32 [1024, 1], P('sector'), may hold values from 0 to 31; in each aligned block of 32 rows (0 to 31, 32 to 63, ...) at most 2 rows name the same one
- pair_target: int32 [1024], P('sector'), may hold values from 0 to 7
Outputs:
- sigma: bfloat16 [256, 256, 256], P('sector', 'term')
Inputs may be any that keep to these rules, and one draw needn't show every extreme that they name: `pair_dest`: among the 32 pairs of one sector index, at most 2 name the same owner, a bound that some block reaches.
All inputs are finite; a program needn't handle non-finite values.
Results may differ from a plain program's by a relative error of at most 0.014.
Values may be sent and summed in bfloat16 or wider, within the bound.
A program may use at most 128 MiB of HBM per device.

v0:
```python
import jax
import jax.numpy as jnp
from jax import lax
from jax.sharding import PartitionSpec as P


def shards(psi, left_env, right_env, pair_source, pair_left, pair_right, pair_dest, pair_target):
    owners = lax.axis_size("sector")
    owned = psi.shape[0]
    width = psi.shape[1]
    count = pair_source.shape[0]
    slots_each = max(2, 2 * count // owners)
    slots = owners * slots_each
    left_local = left_env[0]
    right_local = right_env[0]
    terms_here = left_local.shape[1]
    source_blocks = psi[pair_source]
    accum = jnp.zeros((count, width, width), jnp.float32)
    for mpo_term in range(terms_here):
        inner = jnp.einsum(
            "pij,pjk->pik",
            source_blocks,
            right_local[pair_right, mpo_term],
            preferred_element_type=jnp.float32,
        ).astype(jnp.bfloat16)
        accum = accum + jnp.einsum(
            "pij,pjk->pik",
            left_local[pair_left, mpo_term],
            inner,
            preferred_element_type=jnp.float32,
        )
    part = accum.astype(jnp.bfloat16)
    owner_of = pair_dest[:, 0]
    onehot = (owner_of[:, None] == jnp.arange(owners, dtype=jnp.int32)[None, :]).astype(jnp.int32)
    earlier = jnp.cumsum(onehot, axis=0) - onehot
    slot_of = jnp.sum(earlier * onehot, axis=1)
    position = owner_of * slots_each + slot_of
    labels = jnp.full((slots,), -1, jnp.int32).at[position].set(pair_target)
    outgoing = jnp.zeros((slots, width, width), jnp.bfloat16).at[position].set(part)
    arrived, arrived_labels = (
        lax.all_to_all(outgoing, "sector", split_axis=0, concat_axis=0, tiled=True),
        lax.all_to_all(labels, "sector", split_axis=0, concat_axis=0, tiled=True),
    )
    select = (arrived_labels[None, :] == jnp.arange(owned, dtype=jnp.int32)[:, None]).astype(
        jnp.bfloat16
    )
    gathered = jnp.dot(
        select, arrived.reshape(slots, width * width), preferred_element_type=jnp.float32
    )
    summed = lax.psum_scatter(
        gathered.reshape(owned, width, width), "term", scatter_dimension=1, tiled=True
    )
    return summed.astype(jnp.bfloat16)


def solution(mesh):
    placed = (
        P("sector", None, None),
        P("term", "sector", None, None, None),
        P("term", "sector", None, None, None),
        P("sector"),
        P("sector"),
        P("sector"),
        P("sector", None),
        P("sector"),
    )
    return jax.shard_map(
        shards, mesh=mesh, in_specs=placed, out_specs=P("sector", "term", None), check_vma=False
    )
```

profile of v0, /device:TPU:2, one launch (start us, length us, event | category | flops | bytes accessed | tf_op | source)
XLA Modules:
  0.0 365.0 jit_solution(18368833536054200951)
XLA Ops:
  6.5 0.9 fusion.21
  7.5 0.8 select_reduce_fusion
  9.0 0.8 scatter_custom_fusion
  10.5 11.5 %all-to-all-start = ((s32[32,2,1]{1,2,0:T(1,128)}), s32[32,2,1]{1,2,0:T(1,128)S(1)}, u32[]{:S(2)}, u32[]{:S(2)}) async-start(s32[32,2,1]{1,2,0:T(1,128)} %bitcast.3), calls=%async_computation | async-start | bytes 32768 | tf_op jit(solution)/shard_map/all_to_all | solution.py:42
  22.7 2.8 gather_fusion
  25.5 2.8 gather_fusion.7
  28.3 4.4 %gather_fusion.2 = bf16[32,256,256]{2,1,0:T(8,128)(2,1)} fusion(bf16[4,4,256,256]{3,2,1,0:T(8,128)(2,1)} %bitcast.41, s32[32]{0:T(128)S(1)} %get-tuple-element.6), kind=kCustom, calls=%fused_computation.2 | custom fusion | bytes 8388864 | tf_op jit(solution)/shard_map/gather | solution.py:23
  32.6 4.4 %gather_fusion.8 = bf16[32,256,256]{2,1,0:T(8,128)(2,1)} fusion(bf16[4,4,256,256]{3,2,1,0:T(8,128)(2,1)} %bitcast.42, s32[32]{0:T(128)S(1)} %get-tuple-element.10), kind=kCustom, calls=%fused_computation.8 | custom fusion | bytes 8388864 | tf_op jit(solution)/shard_map/gather | solution.py:23
  37.0 2.8 gather_fusion.5
  39.8 4.4 %gather_fusion.6 = bf16[32,256,256]{2,1,0:T(8,128)(2,1)} fusion(bf16[4,4,256,256]{3,2,1,0:T(8,128)(2,1)} %bitcast.43, s32[32]{0:T(128)S(1)} %get-tuple-element.9), kind=kCustom, calls=%fused_computation.6 | custom fusion | bytes 8388864 | tf_op jit(solution)/shard_map/gather | solution.py:23
  44.1 2.8 gather_fusion.3
  46.9 4.4 %gather_fusion.4 = bf16[32,256,256]{2,1,0:T(8,128)(2,1)} fusion(bf16[4,4,256,256]{3,2,1,0:T(8,128)(2,1)} %bitcast.44, s32[32]{0:T(128)S(1)} %get-tuple-element.5), kind=kCustom, calls=%fused_computation.4 | custom fusion | bytes 8388864 | tf_op jit(solution)/shard_map/gather | solution.py:23
  51.3 2.9 gather_fusion.1
  54.2 10.3 %fusion.3 = f32[32,256,256]{2,1,0:T(8,128)} fusion(bf16[32,256,256]{2,1,0:T(8,128)(2,1)} %gather_fusion.7, bf16[32,256,256]{2,1,0:T(8,128)(2,1)} %gather_fusion.1, bf16[32,256,256]{2,1,0:T(8,128)(2,1)} %gather_fusion.8), kind=kOutput, calls=%fused_computation.15 | convolution fusion | flops 2149580800 | bytes 20971520 | tf_op jit(solution)/shard_map/pij,pjk->pik/dot_general | solution.py:26
  64.5 10.2 %fusion.5 = f32[32,256,256]{2,1,0:T(8,128)} fusion(bf16[32,256,256]{2,1,0:T(8,128)(2,1)} %gather_fusion.5, bf16[32,256,256]{2,1,0:T(8,128)(2,1)} %gather_fusion.1, bf16[32,256,256]{2,1,0:T(8,128)(2,1)} %gather_fusion.6), kind=kOutput, calls=%fused_computation.17 | convolution fusion | flops 2149580800 | bytes 20971520 | tf_op jit(solution)/shard_map/pij,pjk->pik/dot_general | solution.py:26
  74.7 10.3 %fusion.7 = f32[32,256,256]{2,1,0:T(8,128)} fusion(bf16[32,256,256]{2,1,0:T(8,128)(2,1)} %gather_fusion.3, bf16[32,256,256]{2,1,0:T(8,128)(2,1)} %gather_fusion.1, bf16[32,256,256]{2,1,0:T(8,128)(2,1)} %gather_fusion.4), kind=kOutput, calls=%fused_computation.19 | convolution fusion | flops 2149580800 | bytes 20971520 | tf_op jit(solution)/shard_map/pij,pjk->pik/dot_general | solution.py:26
  85.0 16.2 %add_convert_fusion = bf16[32,256,256]{2,1,0:T(8,128)(2,1)} fusion(f32[32,256,256]{2,1,0:T(8,128)} %fusion.3, f32[32,256,256]{2,1,0:T(8,128)} %fusion.5, f32[32,256,256]{2,1,0:T(8,128)} %fusion.7, bf16[32,256,256]{2,1,0:T(8,128)(2,1)} %gather_fusion, bf16[32,256,256]{2,1,0:T(8,128)(2,1)} %gather_fusion.1, bf16[32,256,256]{2,1,0:T(8,128)(2,1)} %gather_fusion.2), kind=kOutput, calls=%fused_computation.14 | convolution fusion | flops 2157969408 | bytes 41943040 | tf_op jit(solution)/shard_map/pij,pjk->pik/dot_general | solution.py:26
  101.1 4.2 %broadcast_in_dim.11 = bf16[64,256,256]{2,1,0:T(8,128)(2,1)} broadcast(bf16[]{:T(256)} %constant.3.clone.1), dimensions={} | broadcast | bytes 8388610 | tf_op jit(solution)/shard_map/broadcast_in_dim | solution.py:39
  105.4 11.4 %scatter_fusion = bf16[64,256,256]{2,1,0:T(8,128)(2,1)} fusion(bf16[64,256,256]{2,1,0:T(8,128)(2,1)} %broadcast_in_dim.11, s32[32]{0:T(128)S(1)} %fusion.25, bf16[32,256,256]{2,1,0:T(8,128)(2,1)} %add_convert_fusion), kind=kCustom, calls=%fused_computation.10 | custom fusion | bytes 12583040 | tf_op jit(solution)/shard_map/scatter | solution.py:39
  116.7 10.0 %all-to-all-start.1 = ((bf16[64,256,256]{2,1,0:T(8,128)(2,1)}), bf16[64,256,256]{2,1,0:T(8,128)(2,1)}, u32[]{:S(2)}, u32[]{:S(2)}) async-start(bf16[64,256,256]{2,1,0:T(8,128)(2,1)} %scatter_fusion), calls=%async_computation.1 | async-start | bytes 16777216 | tf_op jit(solution)/shard_map/all_to_all | solution.py:41
  128.1 184.5 %all-to-all-done.1 = bf16[64,256,256]{2,1,0:T(8,128)(2,1)} async-done(((bf16[64,256,256]{2,1,0:T(8,128)(2,1)}), bf16[64,256,256]{2,1,0:T(8,128)(2,1)}, u32[]{:S(2)}, u32[]{:S(2)}) %all-to-all-start.1) | async-done | bytes 8388640 | tf_op jit(solution)/shard_map/all_to_all | solution.py:41
  312.5 9.4 %fusion = f32[8,256,256]{2,0,1:T(8,128)} fusion(s32[64]{0:T(128)S(1)} %eq.34, bf16[8,8,256,256]{3,2,1,0:T(8,128)(2,1)} %bitcast.10), kind=kOutput, calls=%fused_computation.11 | convolution fusion | flops 67109376 | bytes 10486016 | tf_op jit(solution)/shard_map/dot_general | solution.py:47
  322.0 34.5 %reduce-scatter.2.cloned.1.call-done = f32[8,32,256]{2,0,1:T(8,128)} async-done(((f32[8,256,256]{2,0,1:T(8,128)}), f32[8,32,256]{2,0,1:T(8,128)}) %reduce-scatter.2.cloned.1.call-update) | async-done | bytes 262160 | tf_op jit(solution)/shard_map/reduce_scatter | solution.py:50
  356.5 1.0 convert_element_type.28
  (26 shorter events, 4.2 us)
Async XLA Ops:
  6.5 16.1 %copy-start = (bf16[1,4,4,256,256]{4,3,2,1,0:T(8,128)(2,1)S(1)}, bf16[1,4,4,256,256]{4,3,2,1,0:T(8,128)(2,1)}, u32[]{:S(2)}) copy-start(bf16[1,4,4,256,256]{4,3,2,1,0:T(8,128)(2,1)} %param.9) | copy-start | bytes 6291460
  10.5 106.2 %all-to-all-start = ((s32[32,2,1]{1,2,0:T(1,128)}), s32[32,2,1]{1,2,0:T(1,128)S(1)}, u32[]{:S(2)}, u32[]{:S(2)}) async-start(s32[32,2,1]{1,2,0:T(1,128)} %bitcast.3), calls=%async_computation | async-start | bytes 32768 | tf_op jit(solution)/shard_map/all_to_all | solution.py:42
  25.5 2.8 copy-start.3
  32.6 4.4 %copy-start.4 = (s32[32]{0:T(128)S(1)}, s32[32]{0:T(128)}, u32[]{:S(2)}) copy-start(s32[32]{0:T(128)} %param.11) | copy-start | bytes 388
  46.9 4.4 %copy-start.2 = (bf16[8,256,256]{2,1,0:T(8,128)(2,1)S(1)}, bf16[8,256,256]{2,1,0:T(8,128)(2,1)}, u32[]{:S(2)}) copy-start(bf16[8,256,256]{2,1,0:T(8,128)(2,1)} %param.8) | copy-start | bytes 3145732
  116.7 195.8 %all-to-all-start.1 = ((bf16[64,256,256]{2,1,0:T(8,128)(2,1)}), bf16[64,256,256]{2,1,0:T(8,128)(2,1)}, u32[]{:S(2)}, u32[]{:S(2)}) async-start(bf16[64,256,256]{2,1,0:T(8,128)(2,1)} %scatter_fusion), calls=%async_computation.1 | async-start | bytes 16777216 | tf_op jit(solution)/shard_map/all_to_all | solution.py:41
  126.7 229.8 %reduce-scatter.2.cloned.1.call-start = ((), (), s32[]{:S(2)}) async-start(), calls=%async_computation.3 | async-start | bytes 2359296 | tf_op jit(solution)/shard_map/reduce_scatter | solution.py:50
  312.5 45.6 %copy-start.1 = (bf16[1,4,4,256,256]{4,3,2,1,0:T(8,128)(2,1)S(1)}, bf16[1,4,4,256,256]{4,3,2,1,0:T(8,128)(2,1)}, u32[]{:S(2)}) copy-start(bf16[1,4,4,256,256]{4,3,2,1,0:T(8,128)(2,1)} %param.9) | copy-start | bytes 6291460
Sparse Core Ops, SparseCore 0:
  322.1 34.3 reduce-scatter.1
where the time goes:
time: 369 us; the launch traced here: 365 us
  waiting for transfers between devices  219 us (59%)
  matrix products  56.4 us (15%)
  local copies, waits for them, and re-layouts  49.9 us (14%)
  starting transfers between devices  21.5 us (6%)
  between operations  13.5 us (4%)
  other arithmetic  4.77 us (1%)
    all_to_all x1, waiting for transfers between devices, shards(): lax.all_to_all(outgoing, 'sector', split_axis=0, concat_axis=0, tiled=True)  184 us
    dot_general x4, matrix products, shards(): jnp.einsum('pij,pjk->pik', left_local[pair_left, mpo_term], inner, prefer...  46.9 us
    reduce_scatter x1, waiting for transfers between devices, shards(): lax.psum_scatter(gathered.reshape(owned, width, width), 'term', scatter_d...  34.5 us
    gather x4, local copies, waits for them, and re-layouts, shards(): right_local[pair_right, mpo_term]  17.5 us
    all_to_all x1, starting transfers between devices, shards(): lax.all_to_all(labels, 'sector', split_axis=0, concat_axis=0, tiled=True)  11.5 us
    scatter x1, local copies, waits for them, and re-layouts, shards(): jnp.zeros((slots, width, width), jnp.bfloat16).at[position].set(part)  11.4 us
    gather x4, local copies, waits for them, and re-layouts, shards(): left_local[pair_left, mpo_term]  11.1 us
    all_to_all x1, starting transfers between devices, shards(): lax.all_to_all(outgoing, 'sector', split_axis=0, concat_axis=0, tiled=True)  9.96 us
  transfers between devices with their start and end apart: 3, of which 2 were waited for; matrix products, arithmetic and copies ran while one was open for 26% of the time, Pallas kernels for 0%

commit v1 on v0

--- a/solution.py
+++ b/solution.py
@@ -30,13 +30,15 @@
             preferred_element_type=jnp.float32,
         )
     part = accum.astype(jnp.bfloat16)
+    mine = lax.psum_scatter(part, "term", scatter_dimension=1, tiled=True)
+    rows = mine.shape[1]
     owner_of = pair_dest[:, 0]
     onehot = (owner_of[:, None] == jnp.arange(owners, dtype=jnp.int32)[None, :]).astype(jnp.int32)
     earlier = jnp.cumsum(onehot, axis=0) - onehot
     slot_of = jnp.sum(earlier * onehot, axis=1)
     position = owner_of * slots_each + slot_of
     labels = jnp.full((slots,), -1, jnp.int32).at[position].set(pair_target)
-    outgoing = jnp.zeros((slots, width, width), jnp.bfloat16).at[position].set(part)
+    outgoing = jnp.zeros((slots, rows, width), jnp.bfloat16).at[position].set(mine)
     arrived, arrived_labels = (
         lax.all_to_all(outgoing, "sector", split_axis=0, concat_axis=0, tiled=True),
         lax.all_to_all(labels, "sector", split_axis=0, concat_axis=0, tiled=True),
@@ -45,12 +47,9 @@
         jnp.bfloat16
     )
     gathered = jnp.dot(
-        select, arrived.reshape(slots, width * width), preferred_element_type=jnp.float32
+        select, arrived.reshape(slots, rows * width), preferred_element_type=jnp.float32
     )
-    summed = lax.psum_scatter(
-        gathered.reshape(owned, width, width), "term", scatter_dimension=1, tiled=True
-    )
-    return summed.astype(jnp.bfloat16)
+    return gathered.reshape(owned, rows, width).astype(jnp.bfloat16)
 
 
 def solution(mesh):

time: 369 us -> 181 us (0.49)
  waiting for transfers between devices: 219 us -> 53.9 us
  matrix products: 56.4 us -> 47.6 us
  local copies, waits for them, and re-layouts: 49.9 us -> 41.6 us
    all_to_all x1, waiting for transfers between devices: 184 us -> 27.6 us  [shards(): lax.all_to_all(outgoing, 'sector', split_axis=0, concat_axis=0, tiled=True)]
    dot_general x1, matrix products: 9.44 us -> 0.66 us  [shards(): jnp.dot(select, arrived.reshape(slots, rows * width), preferred_element_t...]
    reduce_scatter x1, waiting for transfers between devices: 34.5 us -> 26.3 us  [shards(): mine = lax.psum_scatter(part, 'term', scatter_dimension=1, tiled=True)]
    scatter x1, local copies, waits for them, and re-layouts: 11.4 us -> 4.82 us  [shards(): jnp.zeros((slots, rows, width), jnp.bfloat16).at[position].set(mine)]
  transfers between devices with their start and end apart: 3 -> 3, of which waited for: 2 -> 2; matrix products, arithmetic and copies ran while one was open for 26% -> 5% of each run, Pallas kernels for 0% -> 0%
where the time goes in v1:
time: 181 us; the launch traced here: 179 us
  waiting for transfers between devices  53.9 us (30%)
  matrix products  47.6 us (26%)
  local copies, waits for them, and re-layouts  41.6 us (23%)
  starting transfers between devices  21 us (12%)
  between operations  13.5 us (7%)
  other arithmetic  1.84 us (1%)
    dot_general x4, matrix products, shards(): jnp.einsum('pij,pjk->pik', left_local[pair_left, mpo_term], inner, prefer...  46.9 us
    all_to_all x1, waiting for transfers between devices, shards(): lax.all_to_all(outgoing, 'sector', split_axis=0, concat_axis=0, tiled=True)  27.6 us
    reduce_scatter x1, waiting for transfers between devices, shards(): mine = lax.psum_scatter(part, 'term', scatter_dimension=1, tiled=True)  26.3 us
    gather x4, local copies, waits for them, and re-layouts, shards(): right_local[pair_right, mpo_term]  17.5 us
    all_to_all x1, starting transfers between devices, shards(): lax.all_to_all(labels, 'sector', split_axis=0, concat_axis=0, tiled=True)  11.5 us
    gather x4, local copies, waits for them, and re-layouts, shards(): left_local[pair_left, mpo_term]  11.1 us
    all_to_all x1, starting transfers between devices, shards(): lax.all_to_all(outgoing, 'sector', split_axis=0, concat_axis=0, tiled=True)  9.55 us
    scatter x1, local copies, waits for them, and re-layouts, shards(): jnp.zeros((slots, rows, width), jnp.bfloat16).at[position].set(mine)  4.82 us
  transfers between devices with their start and end apart: 3, of which 2 were waited for; matrix products, arithmetic and copies ran while one was open for 5% of the time, Pallas kernels for 0%

profile of v1, /device:TPU:2, one launch (start us, length us, event | category | flops | bytes accessed | tf_op | source)
XLA Modules:
  0.0 179.4 jit_solution(2454776813953251825)
XLA Ops:
  6.5 0.8 broadcast_or_fusion.5
  7.4 0.8 copy-done
  8.1 2.8 %gather_fusion = bf16[32,256,256]{2,1,0:T(8,128)(2,1)} fusion(bf16[4,4,256,256]{3,2,1,0:T(8,128)(2,1)S(1)} %bitcast.37, s32[32]{0:T(128)S(1)} %get-tuple-element.8), kind=kCustom, calls=%fused_computation | custom fusion | bytes 8388864 | tf_op jit(solution)/shard_map/gather | solution.py:28
  10.9 2.8 %gather_fusion.7 = bf16[32,256,256]{2,1,0:T(8,128)(2,1)} fusion(bf16[4,4,256,256]{3,2,1,0:T(8,128)(2,1)S(1)} %bitcast.40, s32[32]{0:T(128)S(1)} %get-tuple-element.12), kind=kCustom, calls=%fused_computation.7 | custom fusion | bytes 8388864 | tf_op jit(solution)/shard_map/gather | solution.py:28
  13.7 4.4 %gather_fusion.2 = bf16[32,256,256]{2,1,0:T(8,128)(2,1)} fusion(bf16[4,4,256,256]{3,2,1,0:T(8,128)(2,1)} %bitcast.41, s32[32]{0:T(128)S(1)} %get-tuple-element.6), kind=kCustom, calls=%fused_computation.2 | custom fusion | bytes 8388864 | tf_op jit(solution)/shard_map/gather | solution.py:23
  18.1 4.4 %gather_fusion.8 = bf16[32,256,256]{2,1,0:T(8,128)(2,1)} fusion(bf16[4,4,256,256]{3,2,1,0:T(8,128)(2,1)} %bitcast.42, s32[32]{0:T(128)S(1)} %get-tuple-element.10), kind=kCustom, calls=%fused_computation.8 | custom fusion | bytes 8388864 | tf_op jit(solution)/shard_map/gather | solution.py:23
  22.5 2.7 %gather_fusion.5 = bf16[32,256,256]{2,1,0:T(8,128)(2,1)} fusion(bf16[4,4,256,256]{3,2,1,0:T(8,128)(2,1)S(1)} %bitcast.39, s32[32]{0:T(128)S(1)} %get-tuple-element.11), kind=kCustom, calls=%fused_computation.5 | custom fusion | bytes 8388864 | tf_op jit(solution)/shard_map/gather | solution.py:28
  25.2 4.4 %gather_fusion.6 = bf16[32,256,256]{2,1,0:T(8,128)(2,1)} fusion(bf16[4,4,256,256]{3,2,1,0:T(8,128)(2,1)} %bitcast.43, s32[32]{0:T(128)S(1)} %get-tuple-element.9), kind=kCustom, calls=%fused_computation.6 | custom fusion | bytes 8388864 | tf_op jit(solution)/shard_map/gather | solution.py:23
  29.6 2.8 %gather_fusion.3 = bf16[32,256,256]{2,1,0:T(8,128)(2,1)} fusion(bf16[4,4,256,256]{3,2,1,0:T(8,128)(2,1)S(1)} %bitcast.38, s32[32]{0:T(128)S(1)} %get-tuple-element.7), kind=kCustom, calls=%fused_computation.3 | custom fusion | bytes 8388864 | tf_op jit(solution)/shard_map/gather | solution.py:28
  32.3 4.4 %gather_fusion.4 = bf16[32,256,256]{2,1,0:T(8,128)(2,1)} fusion(bf16[4,4,256,256]{3,2,1,0:T(8,128)(2,1)} %bitcast.44, s32[32]{0:T(128)S(1)} %get-tuple-element.5), kind=kCustom, calls=%fused_computation.4 | custom fusion | bytes 8388864 | tf_op jit(solution)/shard_map/gather | solution.py:23
  36.8 2.8 %gather_fusion.1 = bf16[32,256,256]{2,1,0:T(8,128)(2,1)} fusion(bf16[8,256,256]{2,1,0:T(8,128)(2,1)S(1)} %copy-done.2, s32[1024]{0:T(1024)S(1)} %pad_clamp_fusion), kind=kCustom, calls=%fused_computation.1 | custom fusion | bytes 8388736 | tf_op jit(solution)/shard_map/gather | solution.py:17
  39.6 10.3 %fusion = f32[32,256,256]{2,1,0:T(8,128)} fusion(bf16[32,256,256]{2,1,0:T(8,128)(2,1)} %gather_fusion.7, bf16[32,256,256]{2,1,0:T(8,128)(2,1)} %gather_fusion.1, bf16[32,256,256]{2,1,0:T(8,128)(2,1)} %gather_fusion.8), kind=kOutput, calls=%fused_computation.12 | convolution fusion | flops 2149580800 | bytes 20971520 | tf_op jit(solution)/shard_map/pij,pjk->pik/dot_general | solution.py:26
  49.9 10.3 %fusion.2 = f32[32,256,256]{2,1,0:T(8,128)} fusion(bf16[32,256,256]{2,1,0:T(8,128)(2,1)} %gather_fusion.5, bf16[32,256,256]{2,1,0:T(8,128)(2,1)} %gather_fusion.1, bf16[32,256,256]{2,1,0:T(8,128)(2,1)} %gather_fusion.6), kind=kOutput, calls=%fused_computation.14 | convolution fusion | flops 2149580800 | bytes 20971520 | tf_op jit(solution)/shard_map/pij,pjk->pik/dot_general | solution.py:26
  60.1 10.3 %fusion.4 = f32[32,256,256]{2,1,0:T(8,128)} fusion(bf16[32,256,256]{2,1,0:T(8,128)(2,1)} %gather_fusion.3, bf16[32,256,256]{2,1,0:T(8,128)(2,1)} %gather_fusion.1, bf16[32,256,256]{2,1,0:T(8,128)(2,1)} %gather_fusion.4), kind=kOutput, calls=%fused_computation.16 | convolution fusion | flops 2149580800 | bytes 20971520 | tf_op jit(solution)/shard_map/pij,pjk->pik/dot_general | solution.py:26
  70.4 16.1 %add_convert_fusion = bf16[32,256,256]{2,1,0:T(8,128)(2,1)} fusion(f32[32,256,256]{2,1,0:T(8,128)} %fusion, f32[32,256,256]{2,1,0:T(8,128)} %fusion.2, f32[32,256,256]{2,1,0:T(8,128)} %fusion.4, bf16[32,256,256]{2,1,0:T(8,128)(2,1)} %gather_fusion, bf16[32,256,256]{2,1,0:T(8,128)(2,1)} %gather_fusion.1, bf16[32,256,256]{2,1,0:T(8,128)(2,1)} %gather_fusion.2), kind=kOutput, calls=%fused_computation.11 | convolution fusion | flops 2157969408 | bytes 41943040 | tf_op jit(solution)/shard_map/pij,pjk->pik/dot_general | solution.py:26
  87.5 0.8 scatter_custom_fusion
  88.3 0.7 all_to_all.9
  89.0 11.5 %all-to-all-start = ((s32[32,2,1]{1,2,0:T(1,128)}), s32[32,2,1]{1,2,0:T(1,128)S(1)}, u32[]{:S(2)}, u32[]{:S(2)}) async-start(s32[32,2,1]{1,2,0:T(1,128)} %bitcast.3), calls=%async_computation | async-start | bytes 32768 | tf_op jit(solution)/shard_map/all_to_all | solution.py:44
  100.5 26.3 %reduce-scatter.2.cloned.1.call-done = bf16[32,32,256]{2,1,0:T(8,128)(2,1)} async-done(((bf16[32,256,256]{2,1,0:T(8,128)(2,1)}), bf16[32,32,256]{2,1,0:T(8,128)(2,1)}) %reduce-scatter.2.cloned.1.call-update) | async-done | bytes 524304 | tf_op jit(solution)/shard_map/reduce_scatter | solution.py:33
  126.8 1.1 broadcast_in_dim.11
  128.0 4.8 %scatter_fusion = bf16[64,32,256]{2,1,0:T(8,128)(2,1)} fusion(bf16[64,32,256]{2,1,0:T(8,128)(2,1)} %broadcast_in_dim.11, s32[32]{0:T(128)S(1)} %fusion.24, bf16[32,32,256]{2,1,0:T(8,128)(2,1)} %reduce-scatter.2.cloned.1.call-done), kind=kCustom, calls=%fused_computation.10 | custom fusion | bytes 1572992 | tf_op jit(solution)/shard_map/scatter | solution.py:41
  132.8 9.5 %all-to-all-start.1 = ((bf16[64,32,256]{2,1,0:T(8,128)(2,1)}), bf16[64,32,256]{2,1,0:T(8,128)(2,1)S(1)}, u32[]{:S(2)}, u32[]{:S(2)}) async-start(bf16[64,32,256]{2,1,0:T(8,128)(2,1)} %scatter_fusion), calls=%async_computation.2 | async-start | bytes 2097152 | tf_op jit(solution)/shard_map/all_to_all | solution.py:43
  142.8 0.7 reduce.3
  143.6 27.6 %all-to-all-done.1 = bf16[64,32,256]{2,1,0:T(8,128)(2,1)S(1)} async-done(((bf16[64,32,256]{2,1,0:T(8,128)(2,1)}), bf16[64,32,256]{2,1,0:T(8,128)(2,1)S(1)}, u32[]{:S(2)}, u32[]{:S(2)}) %all-to-all-start.1) | async-done | bytes 1048608 | tf_op jit(solution)/shard_map/all_to_all | solution.py:43
  (27 shorter events, 3.0 us)
Async XLA Ops:
  6.5 1.6 copy-start
  6.5 120.3 %reduce-scatter.2.cloned.1.call-start = ((), (), s32[]{:S(2)}) async-start(), calls=%async_computation.3 | async-start | bytes 4718592 | tf_op jit(solution)/shard_map/reduce_scatter | solution.py:33
  10.9 2.8 %copy-start.4 = (s32[32]{0:T(128)S(1)}, s32[32]{0:T(128)}, u32[]{:S(2)}) copy-start(s32[32]{0:T(128)} %param.13) | copy-start | bytes 388
  18.1 4.4 %copy-start.5 = (s32[32]{0:T(128)S(1)}, s32[32]{0:T(128)}, u32[]{:S(2)}) copy-start(s32[32]{0:T(128)} %param.11) | copy-start | bytes 388
  32.3 4.4 %copy-start.2 = (bf16[8,256,256]{2,1,0:T(8,128)(2,1)S(1)}, bf16[8,256,256]{2,1,0:T(8,128)(2,1)}, u32[]{:S(2)}) copy-start(bf16[8,256,256]{2,1,0:T(8,128)(2,1)} %param.8) | copy-start | bytes 3145732
  86.5 0.7 copy-start.3
  86.6 86.0 %copy-start.1 = (bf16[1,4,4,256,256]{4,3,2,1,0:T(8,128)(2,1)S(1)}, bf16[1,4,4,256,256]{4,3,2,1,0:T(8,128)(2,1)}, u32[]{:S(2)}) copy-start(bf16[1,4,4,256,256]{4,3,2,1,0:T(8,128)(2,1)} %param.9) | copy-start | bytes 6291460
  89.0 43.7 %all-to-all-start = ((s32[32,2,1]{1,2,0:T(1,128)}), s32[32,2,1]{1,2,0:T(1,128)S(1)}, u32[]{:S(2)}, u32[]{:S(2)}) async-start(s32[32,2,1]{1,2,0:T(1,128)} %bitcast.3), calls=%async_computation | async-start | bytes 32768 | tf_op jit(solution)/shard_map/all_to_all | solution.py:44
  132.8 38.4 %all-to-all-start.1 = ((bf16[64,32,256]{2,1,0:T(8,128)(2,1)}), bf16[64,32,256]{2,1,0:T(8,128)(2,1)S(1)}, u32[]{:S(2)}, u32[]{:S(2)}) async-start(bf16[64,32,256]{2,1,0:T(8,128)(2,1)} %scatter_fusion), calls=%async_computation.2 | async-start | bytes 2097152 | tf_op jit(solution)/shard_map/all_to_all | solution.py:43
Sparse Core Ops, SparseCore 0:
  86.7 40.1 reduce-scatter.1

commit v2 on v1

v2 whole, which is shorter than its diff:
```python
import jax
import jax.numpy as jnp
from jax import lax
from jax.experimental import pallas as pl
from jax.experimental.pallas import tpu as pltpu
from jax.sharding import PartitionSpec as P

MESH = pl.DeviceIdType.MESH
F32, BF16, I32 = jnp.float32, jnp.bfloat16, jnp.int32

NX, NCORE, NY, NZ = 4, 2, 4, 8
PAIRS, TERMS, OWNED, WIDTH = 32, 4, 8, 256
ROWS = 16
BATCH = 4
NB = PAIRS // BATCH
LEFT, RIGHT = 0, 1


def kernel(
    psi_hbm, left_hbm, right_hbm, src_hbm, lft_hbm, rgt_hbm, dest_hbm, tgt_hbm,
    out_ref,
    psi, lenv, renv, src_s, lft_s, rgt_s, dest_s, tgt_s,
    inner, part, core_in, a_out, a_in, b_out, b_in, y0, y1, dens, z_out, z_in,
    dcol, tcol, meta, meta_s,
    load_sem, meta_sem, meta_send, meta_recv,
    core_send, core_recv, a_send, a_recv, b_send, b_recv,
    y1_send, y1_recv, y2_send, y2_recv, z_send, z_recv,
):
    term, sector = lax.axis_index("term"), lax.axis_index("sector")
    x, c = term // NCORE, term % NCORE
    y, z = sector // NZ, sector % NZ
    yv = (y0, y1)

    def at_x(d):
        return (((x + d) % NX) * NCORE + c, sector)

    def at_y(d):
        return (term, ((y + d) % NY) * NZ + z)

    def at_z(d):
        return (term, y * NZ + (z + d) % NZ)

    partner = (x * NCORE + 1 - c, sector)
    x_dev = (at_x(NX - 1), at_x(1))
    y_dev = (at_y(NY - 1), at_y(1))
    z_dev = (at_z(NZ - 1), at_z(1))

    small = [(src_hbm, src_s), (lft_hbm, lft_s), (rgt_hbm, rgt_s), (dest_hbm, dest_s), (tgt_hbm, tgt_s)]
    loads = small + [(psi_hbm, psi), (right_hbm, renv), (left_hbm, lenv)]
    loads = [pltpu.make_async_copy(a, b, load_sem.at[i]) for i, (a, b) in enumerate(loads)]
    for cp in loads:
        cp.start()

    barrier = pltpu.get_barrier_semaphore()
    peers = (partner,) + x_dev + y_dev + (at_y(2),) + z_dev
    for dev in peers:
        pl.semaphore_signal(barrier, inc=1, device_id=dev, device_id_type=MESH)

    def remote(src, dst, send, recv, dev):
        return pltpu.make_async_remote_copy(
            src_ref=src, dst_ref=dst, send_sem=send, recv_sem=recv, device_id=dev, device_id_type=MESH
        )

    def first(b):
        for j in range(BATCH):
            p = b * BATCH + j
            rows = psi[src_s[p]]
            r = rgt_s[p]
            for k in range(TERMS):
                inner[p, k] = jnp.dot(rows, renv[r, k], preferred_element_type=F32).astype(BF16)

    def second(h, b):
        t = h * NB + b
        for j in range(BATCH):
            p = b * BATCH + j
            l = lft_s[p]
            acc = None
            for k in range(TERMS):
                lhs = lenv[l, k, :, h].reshape(NX * NCORE * ROWS, WIDTH)
                d = jnp.dot(lhs, inner[p, k], preferred_element_type=F32)
                acc = d if acc is None else acc + d
            for xx in range(NX):
                for cc in range(NCORE):
                    r = (xx * NCORE + cc) * ROWS
                    part[cc, t, xx, j] = acc[r : r + ROWS].astype(BF16)

    def core_copy(t):
        return remote(part.at[1 - c, t], core_in.at[t], core_send.at[t], core_recv.at[t], partner)

    def a_copy(t, d):
        return remote(a_out.at[t, d], a_in.at[t, d], a_send.at[t, d], a_recv.at[t, d], x_dev[d])

    def b_copy(t, d):
        return remote(b_out.at[t, d], b_in.at[t, d], b_send.at[t, d], b_recv.at[t, d], x_dev[d])

    def y1_copy(h, b, d):
        t = h * NB + b
        ps = pl.ds(b * BATCH, BATCH)
        return remote(yv[h].at[0, ps], yv[h].at[3 if d == LEFT else 1, ps], y1_send.at[t, d], y1_recv.at[t, d], y_dev[d])

    def y2_copy(h, b, d):
        t = h * NB + b
        ps = pl.ds(b * BATCH + (BATCH // 2 if d == LEFT else 0), BATCH // 2)
        return remote(
            yv[h].at[3 if d == LEFT else 1, ps], yv[h].at[2, ps], y2_send.at[t, d], y2_recv.at[t, d], y_dev[d]
        )

    def chip_sum(t, d, lo, hi):
        xx = (x + d) % NX
        return part[c, t, xx, lo:hi].astype(F32) + core_in[t, xx, lo:hi].astype(F32)

    half = BATCH // 2

    def stage1(t):
        core_copy(t).wait_recv()
        a_out[t, LEFT] = chip_sum(t, 2, 0, half).astype(BF16)
        a_out[t, RIGHT] = chip_sum(t, 2, half, BATCH).astype(BF16)
        a_copy(t, LEFT).start()
        a_copy(t, RIGHT).start()

    def stage2(t):
        a_copy(t, LEFT).wait_recv()
        a_copy(t, RIGHT).wait_recv()
        b_out[t, LEFT, :half] = (chip_sum(t, 3, 0, half) + a_in[t, LEFT].astype(F32)).astype(BF16)
        b_out[t, LEFT, half:] = chip_sum(t, 3, half, BATCH).astype(BF16)
        b_out[t, RIGHT, :half] = chip_sum(t, 1, 0, half).astype(BF16)
        b_out[t, RIGHT, half:] = (chip_sum(t, 1, half, BATCH) + a_in[t, RIGHT].astype(F32)).astype(BF16)
        b_copy(t, LEFT).start()
        b_copy(t, RIGHT).start()

    def stage3(h, b):
        t = h * NB + b
        b_copy(t, LEFT).wait_recv()
        b_copy(t, RIGHT).wait_recv()
        total = chip_sum(t, 0, 0, BATCH) + b_in[t, LEFT].astype(F32) + b_in[t, RIGHT].astype(F32)
        yv[h][0, pl.ds(b * BATCH, BATCH)] = total.astype(BF16)
        y1_copy(h, b, LEFT).start()
        y1_copy(h, b, RIGHT).start()

    def stage4(h, b):
        y1_copy(h, b, LEFT).wait_recv()
        y1_copy(h, b, RIGHT).wait_recv()
        y2_copy(h, b, LEFT).start()
        y2_copy(h, b, RIGHT).start()

    def y2_wait(h):
        def body(b, _):
            y2_copy(h, b, LEFT).wait_recv()
            y2_copy(h, b, RIGHT).wait_recv()
            return 0

        lax.fori_loop(0, NB, body, 0)

    def densify(h, dz, slot):
        o = y * NZ + (z + dz) % NZ
        blocks, labels = [], []
        for r in range(NY):
            for q in range(2):
                blocks.append(yv[h][r, meta_s[r, q, o]].astype(F32))
                labels.append(meta_s[r, 2 + q, o])
        for t in range(OWNED):
            acc = None
            for blk, lab in zip(blocks, labels):
                term_ = blk * jnp.where(lab == t, 1.0, 0.0).astype(F32)
                acc = term_ if acc is None else acc + term_
            dens[slot, t] = acc

    HALF_T = OWNED // 2

    def z_copy(h, hop, d):
        ts = pl.ds(0, OWNED) if hop else pl.ds(HALF_T if d == LEFT else 0, HALF_T)
        return remote(
            z_out.at[h, hop, d, ts], z_in.at[h, hop, d, ts], z_send.at[h, hop, d], z_recv.at[h, hop, d], z_dev[d]
        )

    def z_step(h, hop):
        if hop == 0:
            densify(h, 4, 0)
            for d in (LEFT, RIGHT):
                ts = slice(HALF_T, OWNED) if d == LEFT else slice(0, HALF_T)
                z_out[h, 0, d, ts] = dens[0, ts].astype(BF16)
                z_copy(h, 0, d).start()
        elif hop < 4:
            densify(h, (4 + hop) % NZ, LEFT)
            densify(h, 4 - hop, RIGHT)
            for d in (LEFT, RIGHT):
                z_copy(h, hop - 1, d).wait_recv()
                if hop == 1:
                    ts = slice(HALF_T, OWNED) if d == LEFT else slice(0, HALF_T)
                    no = slice(0, HALF_T) if d == LEFT else slice(HALF_T, OWNED)
                    z_out[h, 1, d, ts] = (dens[d, ts] + z_in[h, 0, d, ts].astype(F32)).astype(BF16)
                    z_out[h, 1, d, no] = dens[d, no].astype(BF16)
                else:
                    z_out[h, hop, d] = (dens[d] + z_in[h, hop - 1, d].astype(F32)).astype(BF16)
                z_copy(h, hop, d).start()
        else:
            densify(h, 0, 0)
            z_copy(h, 3, LEFT).wait_recv()
            z_copy(h, 3, RIGHT).wait_recv()
            total = dens[0] + z_in[h, 3, LEFT].astype(F32) + z_in[h, 3, RIGHT].astype(F32)
            out_ref[:, h * ROWS : (h + 1) * ROWS, :] = total.astype(BF16)

    for cp in loads[:7]:
        cp.wait()
    for p in range(PAIRS):
        dcol[p] = jnp.full((128,), dest_s[p], I32)
        tcol[p] = jnp.full((128,), tgt_s[p], I32)
    lane = lax.broadcasted_iota(I32, (PAIRS, 128), 1)
    prow = lax.broadcasted_iota(I32, (PAIRS, 128), 0)
    same = dcol[...] == lane
    low = jnp.min(jnp.where(same, prow, PAIRS), axis=0, keepdims=True)
    high = jnp.max(jnp.where(same, prow, -1), axis=0, keepdims=True)
    low_t = jnp.max(jnp.where(same & (prow == low), tcol[...], -1), axis=0, keepdims=True)
    high_t = jnp.max(jnp.where(same & (prow == high) & (high > low), tcol[...], -1), axis=0, keepdims=True)
    meta[0] = jnp.zeros((8, 128), I32)
    meta[0, 0:1] = jnp.clip(low, 0, PAIRS - 1)
    meta[0, 1:2] = jnp.clip(high, 0, PAIRS - 1)
    meta[0, 2:3] = low_t
    meta[0, 3:4] = high_t

    first(0)
    loads[7].wait()
    pl.semaphore_wait(barrier, len(peers))

    def meta_copy(r):
        return remote(meta.at[0], meta.at[r], meta_send.at[r], meta_recv.at[r], at_y(r))

    for r in range(1, NY):
        meta_copy(r).start()

    def loop0(b, _):
        second(0, b)
        core_copy(b).start()
        first(b + 1)

        @pl.when(b >= 1)
        def _():
            stage1(b - 1)

        @pl.when(b >= 2)
        def _():
            stage2(b - 2)

        @pl.when(b >= 3)
        def _():
            stage3(0, b - 3)

        @pl.when(b >= 4)
        def _():
            stage4(0, b - 4)

        return 0

    lax.fori_loop(0, NB - 1, loop0, 0)
    second(0, NB - 1)
    core_copy(NB - 1).start()
    stage1(NB - 2)
    stage2(NB - 3)
    stage3(0, NB - 4)
    stage4(0, NB - 5)

    for r in range(1, NY):
        meta_copy(r).wait_recv()
    to_smem = pltpu.make_async_copy(meta, meta_s, meta_sem)
    to_smem.start()
    to_smem.wait()

    def both(b, lag, stage):
        @pl.when(b < lag)
        def _():
            stage(0, b + NB - lag)

        @pl.when(b >= lag)
        def _():
            stage(1, b - lag)

    def loop1(b, _):
        second(1, b)
        core_copy(NB + b).start()
        stage1(NB + b - 1)
        stage2(NB + b - 2)
        both(b, 3, stage3)
        both(b, 4, stage4)

        @pl.when(b == 5)
        def _():
            y2_wait(0)
            z_step(0, 0)

        @pl.when(b == 7)
        def _():
            z_step(0, 1)

        return 0

    lax.fori_loop(0, NB, loop1, 0)
    stage1(2 * NB - 1)
    stage2(2 * NB - 2)
    stage3(1, NB - 3)
    stage4(1, NB - 4)
    stage2(2 * NB - 1)
    stage3(1, NB - 2)
    stage4(1, NB - 3)
    z_step(0, 2)
    stage3(1, NB - 1)
    stage4(1, NB - 2)
    z_step(0, 3)
    stage4(1, NB - 1)
    z_step(0, 4)
    y2_wait(1)
    for hop in range(5):
        z_step(1, hop)

    for r in range(1, NY):
        meta_copy(r).wait_send()

    def sent(b, _):
        for h in range(2):
            t = h * NB + b
            core_copy(t).wait_send()
            for d in (LEFT, RIGHT):
                a_copy(t, d).wait_send()
                b_copy(t, d).wait_send()
                y1_copy(h, b, d).wait_send()
                y2_copy(h, b, d).wait_send()
        return 0

    lax.fori_loop(0, NB, sent, 0)
    for h in range(2):
        for hop in range(4):
            for d in (LEFT, RIGHT):
                z_copy(h, hop, d).wait_send()


def shards(psi, left_env, right_env, pair_source, pair_left, pair_right, pair_dest, pair_target):
    steps = 2 * NB
    block = (ROWS, WIDTH)
    dma = pltpu.SemaphoreType.DMA
    return pl.pallas_call(
        kernel,
        out_shape=jax.ShapeDtypeStruct((OWNED, 2 * ROWS, WIDTH), BF16),
        in_specs=[pl.BlockSpec(memory_space=pl.ANY)] * 8,
        out_specs=pl.BlockSpec(memory_space=pltpu.VMEM),
        scratch_shapes=[
            pltpu.VMEM((OWNED, WIDTH, WIDTH), BF16),
            pltpu.VMEM((4, TERMS, NX * NCORE, 2) + block, BF16),
            pltpu.VMEM((4, TERMS, WIDTH, WIDTH), BF16),
        ]
        + [pltpu.SMEM((PAIRS,), I32)] * 5
        + [
            pltpu.VMEM((PAIRS, TERMS, WIDTH, WIDTH), BF16),
            pltpu.VMEM((NCORE, steps, NX, BATCH) + block, BF16),
            pltpu.VMEM((steps, NX, BATCH) + block, BF16),
            pltpu.VMEM((steps, 2, BATCH // 2) + block, BF16),
            pltpu.VMEM((steps, 2, BATCH // 2) + block, BF16),
            pltpu.VMEM((steps, 2, BATCH) + block, BF16),
            pltpu.VMEM((steps, 2, BATCH) + block, BF16),
            pltpu.VMEM((NY, PAIRS) + block, BF16),
            pltpu.VMEM((NY, PAIRS) + block, BF16),
            pltpu.VMEM((2, OWNED) + block, F32),
            pltpu.VMEM((2, 4, 2, OWNED) + block, BF16),
            pltpu.VMEM((2, 4, 2, OWNED) + block, BF16),
            pltpu.VMEM((PAIRS, 128), I32),
            pltpu.VMEM((PAIRS, 128), I32),
            pltpu.VMEM((NY, 8, 128), I32),
            pltpu.SMEM((NY, 8, 128), I32),
            dma((8,)), dma, dma((NY,)), dma((NY,)),
            dma((steps,)), dma((steps,)),
            dma((steps, 2)), dma((steps, 2)), dma((steps, 2)), dma((steps, 2)),
            dma((steps, 2)), dma((steps, 2)), dma((steps, 2)), dma((steps, 2)),
            dma((2, 4, 2)), dma((2, 4, 2)),
        ],
        compiler_params=pltpu.CompilerParams(
            collective_id=0, has_side_effects=True, vmem_limit_bytes=56 * 2**20
        ),
        name="sigma",
    )(
        psi,
        left_env.reshape((4, TERMS, NX * NCORE, 2) + block),
        right_env.reshape((4, TERMS, WIDTH, WIDTH)),
        pair_source, pair_left, pair_right, pair_dest.reshape(PAIRS), pair_target,
    )


def solution(mesh):
    placed = (
        P("sector", None, None),
        P("term", "sector", None, None, None),
        P("term", "sector", None, None, None),
        P("sector"),
        P("sector"),
        P("sector"),
        P("sector", None),
        P("sector"),
    )
    return jax.shard_map(
        shards, mesh=mesh, in_specs=placed, out_specs=P("sector", "term", None), check_vma=False
    )
```

time: 181 us -> 86.5 us (0.48)
  Pallas kernels: 0 us -> 84.9 us
  waiting for transfers between devices: 53.9 us -> 0 us
  matrix products: 47.6 us -> 0 us
  local copies, waits for them, and re-layouts: 41.6 us -> 1.57 us
  starting transfers between devices: 21 us -> 0 us
  between operations: 13.5 us -> 0.01 us
  other arithmetic: 1.84 us -> 0 us
    pallas_call x0 -> x1, Pallas kernels: none -> 84.9 us  [shards(): pl.pallas_call(kernel, out_shape=jax.ShapeDtypeStruct((OWNED, 2 * ROWS, W...]
    dot_general x5 -> x0, matrix products: 47.6 us -> none  [the longest x4 46.9 us: shards(): jnp.einsum('pij,pjk->pik', left_local[pair_left, mpo_term], inner, prefer...]
    gather x9 -> x0, local copies, waits for them, and re-layouts: 31.4 us -> none  [the longest x4 17.5 us: shards(): right_local[pair_right, mpo_term]]
    all_to_all x2 -> x0, waiting for transfers between devices: 27.6 us -> none  [the longest x1 27.6 us: shards(): lax.all_to_all(outgoing, 'sector', split_axis=0, concat_axis=0, tiled=True)]
    reduce_scatter x1 -> x0, waiting for transfers between devices: 26.3 us -> none  [shards(): mine = lax.psum_scatter(part, 'term', scatter_dimension=1, tiled=True)]
    all_to_all x2 -> x0, starting transfers between devices: 21 us -> none  [the longest x1 11.5 us: shards(): lax.all_to_all(labels, 'sector', split_axis=0, concat_axis=0, tiled=True)]
    scatter x2 -> x0, local copies, waits for them, and re-layouts: 5.63 us -> none  [the longest x1 4.82 us: shards(): jnp.zeros((slots, rows, width), jnp.bfloat16).at[position].set(mine)]
  transfers between devices with their start and end apart: 3 -> 0, of which waited for: 2 -> 0; matrix products, arithmetic and copies ran while one was open for 5% -> 0% of each run, Pallas kernels for 0% -> 0%
where the time goes in v2:
time: 86.5 us; the launch traced here: 86.4 us
  Pallas kernels  84.9 us (98%)
  local copies, waits for them, and re-layouts  1.57 us (2%)
    pallas_call x1, Pallas kernels, shards(): pl.pallas_call(kernel, out_shape=jax.ShapeDtypeStruct((OWNED, 2 * ROWS, W...  84.9 us

profile of v2, /device:TPU:2, one launch (start us, length us, event | category | flops | bytes accessed | tf_op | source)
XLA Modules:
  0.0 86.4 jit_solution(8798031585037939018)
XLA Ops:
  0.0 84.9 %sigma.1 = bf16[8,32,256]{2,1,0:T(8,128)(2,1)} custom-call(bf16[8,256,256]{2,1,0:T(8,128)(2,1)} %psi_hbm.1, bf16[4,4,8,2,16,256]{5,4,3,2,1,0:T(8,128)(2,1)} %bitcast.3, bf16[4,4,256,256]{3,2,1,0:T(8,128)(2,1)} %bitcast.4, s32[32]{0:T(128)} %src_hbm.1, s32[32]{0:T(128)} %lft_hbm.1, s32[32]{0:T(128)} %rgt_hbm.1, s32[32]{0:T(128)} %bitcast.5, s32[32]{0:T(128)} %tgt_hbm.1), custom_call_target="tpu_custom_call" | custom-call | tf_op jit(solution)/shard_map/sigma/pallas_call | solution.py:339
  84.9 1.6 %copy.10 = bf16[8,32,256]{2,1,0:T(8,128)(2,1)} copy(bf16[8,32,256]{2,1,0:T(8,128)(2,1)} %sigma.1) | data formatting | bytes 262144

commit v3 on v1

v3 whole, which is shorter than its diff:
```python
import jax
import jax.numpy as jnp
from jax import lax
from jax.experimental import pallas as pl
from jax.experimental.pallas import tpu as pltpu
from jax.sharding import PartitionSpec as P

MESH = pl.DeviceIdType.MESH
F32, BF16, I32 = jnp.float32, jnp.bfloat16, jnp.int32

NX, NCORE, NY, NZ = 4, 2, 4, 8
NS = NY * NZ
PAIRS, TERMS, OWNED, WIDTH = 32, 4, 8, 256
ROWS = 16
BATCH = 8
NB = PAIRS // BATCH
CAP = 2
GROUPS = ((16, 32), (1, 16))
GROUP = [1] * 16 + [0] * 16
ORDER = [d for lo, hi in GROUPS for d in sorted(range(lo, hi), key=lambda d: abs(d % NZ - NZ // 2))] + [0]


def kernel(
    psi_hbm, left_hbm, right_hbm, src_hbm, lft_hbm, rgt_hbm, dest_hbm, tgt_hbm,
    out_ref,
    psi, lenv, renv, src_s, lft_s, rgt_s, dest_s, tgt_s,
    inner, part, core_in, x_out, x_in, red, slot_out, slot_in,
    dcol, tcol, table_s, tables, labels,
    load_sem, table_sem, ty_send, ty_recv, tz_send, tz_recv,
    core_send, core_recv, x_send, x_recv, s_send, s_recv,
):
    term, sector = lax.axis_index("term"), lax.axis_index("sector")
    x, c = term // NCORE, term % NCORE
    y, z = sector // NZ, sector % NZ

    x_at = [lax.rem(x + d, NX) for d in range(NX)]
    y_at = [lax.rem(y + d, NY) * NZ for d in range(NY)]
    z_at = [lax.rem(z + d, NZ) for d in range(NZ)]

    def at_x(d):
        return (x_at[d] * NCORE + c, sector)

    def owner(d):
        return y_at[d // NZ] + z_at[d % NZ]

    def at_s(d):
        return (term, owner(d))

    partner = (x * NCORE + 1 - c, sector)

    small = [(src_hbm, src_s), (lft_hbm, lft_s), (rgt_hbm, rgt_s), (dest_hbm, dest_s), (tgt_hbm, tgt_s)]
    loads = small + [(psi_hbm, psi), (right_hbm, renv), (left_hbm, lenv)]
    loads = [pltpu.make_async_copy(a, b, load_sem.at[i]) for i, (a, b) in enumerate(loads)]
    for cp in loads:
        cp.start()

    barrier = pltpu.get_barrier_semaphore()

    def greet(dev):
        pl.semaphore_signal(barrier, inc=1, device_id=dev, device_id_type=MESH)

    greet(partner)
    for d in range(1, NX):
        greet(at_x(d))

    for d in range(1, NS):
        greet(at_s(d))

    def remote(src, dst, send, recv, dev):
        return pltpu.make_async_remote_copy(
            src_ref=src, dst_ref=dst, send_sem=send, recv_sem=recv, device_id=dev, device_id_type=MESH
        )

    def compute(b):
        for k in range(TERMS):
            for j in range(BATCH):
                p = b * BATCH + j
                inner[j, k] = jnp.dot(psi[src_s[p]], renv[rgt_s[p], k], preferred_element_type=F32).astype(BF16)
        for j in range(BATCH):
            l = lft_s[b * BATCH + j]
            acc = None
            for k in range(TERMS):
                d = jnp.dot(lenv[l, k], inner[j, k], preferred_element_type=F32)
                acc = d if acc is None else acc + d
            for xx in range(NX):
                for cc in range(NCORE):
                    for h in range(2):
                        r = ((xx * NCORE + cc) * 2 + h) * ROWS
                        part[h, cc, b, xx, j] = acc[r : r + ROWS].astype(BF16)

    def core_copy(h, b):
        return remote(part.at[h, 1 - c, b], core_in.at[h, b], core_send.at[h], core_recv.at[h, b], partner)

    def x_copy(h, b, d):
        return remote(x_out.at[h, b, d - 1], x_in.at[h, b, d - 1], x_send.at[h], x_recv.at[h, b], at_x(d))

    def chip_sum(h, b, d):
        xx = x_at[d]
        return part[h, c, b, xx].astype(F32) + core_in[h, b, xx].astype(F32)

    def stage_x(h, b):
        core_copy(h, b).wait_recv()
        for d in (2, 1, 3):
            x_out[h, b, d - 1] = chip_sum(h, b, d).astype(BF16)
            x_copy(h, b, d).start()

    def stage_sum(h, b):
        remote(x_out.at[h, b], x_in.at[h, b], x_send.at[h], x_recv.at[h, b], at_x(1)).wait_recv()
        total = chip_sum(h, b, 0)
        for d in (1, 2, 3):
            total = total + x_in[h, b, d - 1].astype(F32)
        red[h, pl.ds(b * BATCH, BATCH)] = total.astype(BF16)

    def s_copy(h, d):
        return remote(slot_out.at[h, d], slot_in.at[h, d], s_send.at[h], s_recv.at[h, GROUP[d]], at_s(d))

    def send_slots(h):
        for d in ORDER:
            o = owner(d)
            for q in range(CAP):
                (slot_out if d else slot_in)[h, d, q] = red[h, table_s[q, o]]
            if d:
                s_copy(h, d).start()

    def finish(h):
        acc = [jnp.zeros((ROWS, WIDTH), F32) for _ in range(OWNED)]
        for g, (lo, hi) in enumerate(GROUPS):
            remote(
                slot_out.at[h, lo:hi], slot_in.at[h, lo:hi], s_send.at[h], s_recv.at[h, g], partner
            ).wait_recv()
            for d in range(lo, hi):
                add_slots(h, d, acc)
        add_slots(h, 0, acc)
        for t in range(OWNED):
            out_ref[t, h * ROWS : (h + 1) * ROWS, :] = acc[t].astype(BF16)

    def add_slots(h, d, acc):
        for q in range(CAP):
            blk = slot_in[h, d, q].astype(F32)
            lab = jnp.broadcast_to(labels[d % NZ, d // NZ, 2 + q : 3 + q, :], (ROWS, 128))
            lab = jnp.concatenate([lab, lab], axis=1)
            for t in range(OWNED):
                acc[t] = acc[t] + jnp.where(lab == t, blk, 0.0)

    for cp in loads[:7]:
        cp.wait()
    for p in range(PAIRS):
        dcol[p] = jnp.full((128,), dest_s[p], I32)
        tcol[p] = jnp.full((128,), tgt_s[p], I32)
    lane = lax.broadcasted_iota(I32, (PAIRS, 128), 1)
    prow = lax.broadcasted_iota(I32, (PAIRS, 128), 0)
    same = dcol[...] == lane
    low = jnp.min(jnp.where(same, prow, PAIRS), axis=0, keepdims=True)
    high = jnp.max(jnp.where(same, prow, -1), axis=0, keepdims=True)
    low_t = jnp.max(jnp.where(same & (prow == low), tcol[...], -1), axis=0, keepdims=True)
    high_t = jnp.max(jnp.where(same & (prow == high) & (high > low), tcol[...], -1), axis=0, keepdims=True)
    tables[0, 0] = jnp.concatenate(
        [jnp.clip(low, 0, PAIRS - 1), jnp.clip(high, 0, PAIRS - 1), low_t, high_t, jnp.zeros((4, 128), I32)], axis=0
    )
    to_smem = pltpu.make_async_copy(tables.at[0, 0], table_s, table_sem)
    to_smem.start()
    loads[7].wait()

    compute(0)
    to_smem.wait()
    pl.semaphore_wait(barrier, 1 + NX - 1 + NS - 1)
    core_copy(0, 0).start()
    core_copy(1, 0).start()

    def ty_copy(d):
        return remote(tables.at[0, 0], tables.at[0, d], ty_send, ty_recv.at[d], at_s(d * NZ))

    def tz_copy(d):
        return remote(tables.at[0], tables.at[d], tz_send, tz_recv.at[d], at_s(d))

    for d in range(1, NY):
        ty_copy(d).start()

    def loop(b, _):
        compute(b)
        core_copy(0, b).start()
        core_copy(1, b).start()
        stage_x(0, b - 1)

        @pl.when(b == 2)
        def _():
            for d in range(1, NY):
                ty_copy(d).wait_recv()
            for d in range(1, NZ):
                tz_copy(d).start()

        return 0

    lax.fori_loop(1, NB, loop, 0)
    stage_sum(0, 0)
    stage_x(0, NB - 1)
    for b in range(NB):
        stage_x(1, b)
    for d in range(1, NZ):
        tz_copy(d).wait_recv()
    mine = lax.broadcasted_iota(I32, tables.shape, 3) == sector
    picked = jnp.sum(jnp.where(mine, tables[...], 0), axis=3, keepdims=True)
    labels[...] = jnp.broadcast_to(picked, tables.shape)
    for b in range(1, NB):
        stage_sum(0, b)
    send_slots(0)
    for b in range(NB):
        stage_sum(1, b)
    send_slots(1)
    finish(0)
    finish(1)

    remote(tables.at[0, 1:], tables.at[0, 1:], ty_send, ty_recv.at[1], partner).wait_send()
    remote(tables.at[1:], tables.at[1:], tz_send, tz_recv.at[1], partner).wait_send()
    for h in range(2):
        remote(core_in.at[h], core_in.at[h], core_send.at[h], core_recv.at[h, 0], partner).wait_send()
        remote(x_out.at[h], x_in.at[h], x_send.at[h], x_recv.at[h, 0], partner).wait_send()
        remote(slot_out.at[h, 1:], slot_in.at[h, 1:], s_send.at[h], s_recv.at[h, 0], partner).wait_send()


def shards(psi, left_env, right_env, pair_source, pair_left, pair_right, pair_dest, pair_target):
    block = (ROWS, WIDTH)
    dma = pltpu.SemaphoreType.DMA
    return pl.pallas_call(
        kernel,
        out_shape=jax.ShapeDtypeStruct((OWNED, 2 * ROWS, WIDTH), BF16),
        in_specs=[pl.BlockSpec(memory_space=pl.ANY)] * 8,
        out_specs=pl.BlockSpec(memory_space=pltpu.VMEM),
        scratch_shapes=[
            pltpu.VMEM((OWNED, WIDTH, WIDTH), BF16),
            pltpu.VMEM((4, TERMS, WIDTH, WIDTH), BF16),
            pltpu.VMEM((4, TERMS, WIDTH, WIDTH), BF16),
        ]
        + [pltpu.SMEM((PAIRS,), I32)] * 5
        + [
            pltpu.VMEM((BATCH, TERMS, WIDTH, WIDTH), BF16),
            pltpu.VMEM((2, NCORE, NB, NX, BATCH) + block, BF16),
            pltpu.VMEM((2, NB, NX, BATCH) + block, BF16),
            pltpu.VMEM((2, NB, NX - 1, BATCH) + block, BF16),
            pltpu.VMEM((2, NB, NX - 1, BATCH) + block, BF16),
            pltpu.VMEM((2, PAIRS) + block, BF16),
            pltpu.VMEM((2, NS, CAP) + block, BF16),
            pltpu.VMEM((2, NS, CAP) + block, BF16),
            pltpu.VMEM((PAIRS, 128), I32),
            pltpu.VMEM((PAIRS, 128), I32),
            pltpu.SMEM((8, 128), I32),
            pltpu.VMEM((NZ, NY, 8, 128), I32),
            pltpu.VMEM((NZ, NY, 8, 128), I32),
            dma((8,)), dma, dma, dma((NY,)), dma, dma((NZ,)),
            dma((2,)), dma((2, NB)),
            dma((2,)), dma((2, NB)),
            dma((2,)), dma((2, len(GROUPS))),
        ],
        compiler_params=pltpu.CompilerParams(
            collective_id=0, has_side_effects=True, vmem_limit_bytes=56 * 2**20
        ),
        name="sigma",
    )(
        psi,
        left_env.reshape((4, TERMS, WIDTH, WIDTH)),
        right_env.reshape((4, TERMS, WIDTH, WIDTH)),
        pair_source, pair_left, pair_right, pair_dest.reshape(PAIRS), pair_target,
    )


def solution(mesh):
    placed = (
        P("sector", None, None),
        P("term", "sector", None, None, None),
        P("term", "sector", None, None, None),
        P("sector"),
        P("sector"),
        P("sector"),
        P("sector", None),
        P("sector"),
    )
    return jax.shard_map(
        shards, mesh=mesh, in_specs=placed, out_specs=P("sector", "term", None), check_vma=False
    )
```

time: 181 us -> 56.7 us (0.31)
  the two profiles are of different devices: /device:TPU:2 before, /device:TPU:1 now
where the time goes in v3:
time: 56.7 us; the launch traced here: 56.6 us
  Pallas kernels  55.1 us (97%)
  local copies, waits for them, and re-layouts  1.57 us (3%)
    pallas_call x1, Pallas kernels, shards(): pl.pallas_call(kernel, out_shape=jax.ShapeDtypeStruct((OWNED, 2 * ROWS, W...  55.1 us
    unnamed x1, local copies, waits for them, and re-layouts  1.57 us

profile of v3, /device:TPU:1, one launch (start us, length us, event | category | flops | bytes accessed | tf_op | source)
XLA Modules:
  0.0 56.6 jit_solution(13083102803462890289)
XLA Ops:
  0.0 55.1 %sigma.1 = bf16[8,32,256]{2,1,0:T(8,128)(2,1)} custom-call(bf16[8,256,256]{2,1,0:T(8,128)(2,1)} %psi_hbm.1, bf16[4,4,256,256]{3,2,1,0:T(8,128)(2,1)} %bitcast.3, bf16[4,4,256,256]{3,2,1,0:T(8,128)(2,1)} %bitcast.4, s32[32]{0:T(128)} %src_hbm.1, s32[32]{0:T(128)} %lft_hbm.1, s32[32]{0:T(128)} %rgt_hbm.1, s32[32]{0:T(128)} %bitcast.5, s32[32]{0:T(128)} %tgt_hbm.1), custom_call_target="tpu_custom_call" | custom-call | tf_op jit(solution)/shard_map/sigma/pallas_call | solution.py:224
  55.1 1.6 %copy.10 = bf16[8,32,256]{2,1,0:T(8,128)(2,1)} copy(bf16[8,32,256]{2,1,0:T(8,128)(2,1)} %sigma.1) | data formatting | bytes 262144

commit v4 on v3

v4 whole, which is shorter than its diff:
```python
import jax
import jax.numpy as jnp
from jax import lax
from jax.experimental import pallas as pl
from jax.experimental.pallas import tpu as pltpu
from jax.sharding import PartitionSpec as P

MESH = pl.DeviceIdType.MESH
F32, BF16, I32 = jnp.float32, jnp.bfloat16, jnp.int32

NX, NCORE, NY, NZ = 4, 2, 4, 8
PAIRS, TERMS, OWNED, WIDTH = 32, 4, 8, 256
ROWS, COLS, CHUNKS = 16, 128, 4
BATCH = 4
NB = PAIRS // BATCH
SUB = BATCH // 2
CAP = 2
LEFT, RIGHT = 0, 1
BOTH = (LEFT, RIGHT)
HALF_T = OWNED // 2


def kernel(
    psi_hbm, left_hbm, right_hbm, src_hbm, lft_hbm, rgt_hbm, dest_hbm, tgt_hbm,
    out_ref,
    psi, lenv, renv, src_s, lft_s, rgt_s, dest_s, tgt_s,
    inner, part, core_in, x_out, x_in, a_out, a_in, b_out, b_in, red,
    zslot_out, zslot_in, own, row_out, row_in, slot_out, slot_in, dens, near_out, near_in, far_out, far_in, mid_out, mid_in,
    dcol, tcol, table_s, tables, tables_z, labels, labels_z,
    load_sem, table_sem, table_send, table_recv, table_z_send, table_z_recv,
    core_send, core_recv, x_send, x_recv, a_send, a_recv, b_send, b_recv,
    zs_send, zs_recv, row_send, row_recv, y_send, y_recv, near_send, near_recv, far_send, far_recv, mid_send, mid_recv,
):
    term, sector = lax.axis_index("term"), lax.axis_index("sector")
    x, c = term // NCORE, term % NCORE
    y, z = sector // NZ, sector % NZ
    x_at = [lax.rem(x + d, NX) for d in range(NX)]
    y_at = [lax.rem(y + d, NY) * NZ for d in range(NY)]
    z_at = [lax.rem(z + d, NZ) for d in range(NZ)]

    def at_x(d):
        return (x_at[d] * NCORE + c, sector)

    def at_y(d):
        return (term, y_at[d] + z)

    def at_z(d):
        return (term, y_at[0] + z_at[d])

    partner = (x * NCORE + 1 - c, sector)
    x_dev = (at_x(3), at_x(1))
    z_one = (at_z(7), at_z(1))
    z_two = (at_z(6), at_z(2))

    small = [(src_hbm, src_s), (lft_hbm, lft_s), (rgt_hbm, rgt_s), (dest_hbm, dest_s), (tgt_hbm, tgt_s)]
    loads = small + [(psi_hbm, psi), (right_hbm, renv), (left_hbm, lenv)]
    loads = [pltpu.make_async_copy(a, b, load_sem.at[i]) for i, (a, b) in enumerate(loads)]
    for cp in loads:
        cp.start()

    barrier = pltpu.get_barrier_semaphore()
    peers = [partner] + [at_x(d) for d in (1, 2, 3)] + [at_y(d) for d in (1, 2, 3)]
    peers += [at_z(d) for d in range(1, NZ)]
    for dev in peers:
        pl.semaphore_signal(barrier, inc=1, device_id=dev, device_id_type=MESH)

    def remote(src, dst, send, recv, dev):
        return pltpu.make_async_remote_copy(
            src_ref=src, dst_ref=dst, send_sem=send, recv_sem=recv, device_id=dev, device_id_type=MESH
        )

    def arrived(dst, recv):
        remote(dst, dst, recv, recv, partner).wait_recv()

    def left(src, send):
        remote(src, src, send, send, partner).wait_send()

    def compute(b):
        for k in range(TERMS):
            for j in range(BATCH):
                p = b * BATCH + j
                inner[j, k] = jnp.dot(psi[src_s[p]], renv[rgt_s[p], k], preferred_element_type=F32).astype(BF16)
        for j in range(BATCH):
            l = lft_s[b * BATCH + j]
            acc = None
            for k in range(TERMS):
                d = jnp.dot(lenv[l, k], inner[j, k], preferred_element_type=F32)
                acc = d if acc is None else acc + d
            for xx in range(NX):
                for cc in range(NCORE):
                    for h in range(2):
                        r = ((xx * NCORE + cc) * 2 + h) * ROWS
                        part[h, cc, b, xx, j] = acc[r : r + ROWS].astype(BF16)

    def core_copy(h, b):
        return remote(part.at[h, 1 - c, b], core_in.at[h, b], core_send, core_recv.at[h, b], partner)

    def chip_sum(h, b, d, lo=0, hi=BATCH):
        xx = x_at[d]
        return part[h, c, b, xx, lo:hi].astype(F32) + core_in[h, b, xx, lo:hi].astype(F32)

    def x_copy(b, d):
        return remote(x_out.at[b, d - 1], x_in.at[b, d - 1], x_send, x_recv.at[b], at_x(d))

    def stage_x(b):
        arrived(core_in.at[0, b], core_recv.at[0, b])
        for d in (2, 1, 3):
            x_out[b, d - 1] = chip_sum(0, b, d).astype(BF16)
            x_copy(b, d).start()

    def stage_sum0(b):
        arrived(x_in.at[b], x_recv.at[b])
        total = chip_sum(0, b, 0)
        for d in (1, 2, 3):
            total = total + x_in[b, d - 1].astype(F32)
        red[0, pl.ds(b * BATCH, BATCH)] = total.astype(BF16)

    def stage_a(b):
        arrived(core_in.at[1, b], core_recv.at[1, b])
        for d in BOTH:
            a_out[b, d] = chip_sum(1, b, 2, d * SUB, (d + 1) * SUB).astype(BF16)
            remote(a_out.at[b, d], a_in.at[b, d], a_send, a_recv.at[b], x_dev[d]).start()

    def send_b(ch, lo, hi):
        for d in BOTH:
            ps = pl.ds(lo * BATCH, (hi - lo) * BATCH)
            remote(b_out.at[ch, d, ps], b_in.at[ch, d, ps], b_send, b_recv.at[ch], x_dev[d]).start()

    def stage_b(b):
        arrived(a_in.at[b], a_recv.at[b])
        for d in BOTH:
            total = chip_sum(1, b, 3 if d == LEFT else 1)
            extra = a_in[b, d].astype(F32)
            lo, hi = total[:SUB], total[SUB:]
            if d == LEFT:
                lo = lo + extra
            else:
                hi = hi + extra
            total = jnp.concatenate([lo, hi], axis=0).astype(BF16)
            for ch in range(2):
                b_out[ch, d, pl.ds(b * BATCH, BATCH)] = total[:, :, ch * COLS : (ch + 1) * COLS]

    def stage_sum1(ch):
        arrived(b_in.at[ch], b_recv.at[ch])
        cols = slice(ch * COLS, (ch + 1) * COLS)
        for b in range(NB):
            ps = pl.ds(b * BATCH, BATCH)
            xx = x_at[0]
            total = part[1, c, b, xx, :, :, cols].astype(F32) + core_in[1, b, xx, :, :, cols].astype(F32)
            total = total + b_in[ch, LEFT, ps].astype(F32) + b_in[ch, RIGHT, ps].astype(F32)
            red[1, ps, :, cols] = total.astype(BF16)

    def add_slot(acc, blk, lab):
        blk = blk.astype(F32)
        lab = jnp.broadcast_to(lab, (ROWS, COLS))
        for t in range(OWNED):
            term_ = jnp.where(lab == t, blk, 0.0)
            acc[t] = term_ if acc[t] is None else acc[t] + term_

    def send_z():
        for dz in (4, 3, 5, 2, 6, 1, 7, 0):
            for dy in range(NY):
                o = y_at[dy] + z_at[dz]
                for s in range(CAP):
                    blk = red[0, table_s[s, o], :, :COLS]
                    if dz:
                        zslot_out[dz - 1, dy, s] = blk
                    else:
                        zslot_in[0, dy, s] = blk
            if dz:
                remote(zslot_out.at[dz - 1], zslot_in.at[dz], zs_send, zs_recv, at_z(dz)).start()

    def row_z():
        arrived(zslot_in.at[1:], zs_recv)
        for dy in (2, 1, 3, 0):
            acc = [None] * OWNED
            for dz in range(NZ):
                for s in range(CAP):
                    add_slot(acc, zslot_in[dz, dy, s], labels_z[dy, dz, 2 + s : 3 + s, :])
            for t in range(OWNED):
                if dy:
                    row_out[dy - 1, t] = acc[t].astype(BF16)
                else:
                    own[t] = acc[t]
            if dy:
                remote(row_out.at[dy - 1], row_in.at[dy - 1], row_send, row_recv, at_y(dy)).start()

    def finish_z():
        arrived(row_in, row_recv)
        total = own[...]
        for dy in range(1, NY):
            total = total + row_in[dy - 1].astype(F32)
        out_ref[:, :ROWS, :COLS] = total.astype(BF16)

    def send_y(q):
        h, cols = q // 2, slice((q % 2) * COLS, (q % 2 + 1) * COLS)
        for dy in (2, 1, 3, 0):
            for dz in range(NZ):
                o = y_at[dy] + z_at[dz]
                for s in range(CAP):
                    blk = red[h, table_s[s, o], :, cols]
                    if dy:
                        slot_out[q - 1, dy - 1, dz, s] = blk
                    else:
                        slot_in[q - 1, 0, dz, s] = blk
            if dy:
                remote(slot_out.at[q - 1, dy - 1], slot_in.at[q - 1, dy], y_send, y_recv.at[q - 1], at_y(dy)).start()

    def dense(q, dz):
        acc = [None] * OWNED
        for dy in range(NY):
            for s in range(CAP):
                add_slot(acc, slot_in[q - 1, dy, dz, s], labels[dz, dy, 2 + s : 3 + s, :])
        return acc

    def first_z(q):
        arrived(slot_in.at[q - 1, 1:], y_recv.at[q - 1])
        acc = dense(q, 4)
        for t in range(HALF_T):
            far_out[q - 1, RIGHT, t] = acc[t].astype(BF16)
            far_out[q - 1, LEFT, t] = acc[HALF_T + t].astype(BF16)
        for d in BOTH:
            remote(far_out.at[q - 1, d], far_in.at[q - 1, d], far_send, far_recv.at[q - 1, d], z_two[d]).start()
        for d in BOTH:
            for i, dz in enumerate((1, 3) if d == RIGHT else (7, 5)):
                acc = dense(q, dz)
                for t in range(OWNED):
                    near_out[q - 1, d, i, t] = acc[t].astype(BF16)
            remote(near_out.at[q - 1, d], near_in.at[q - 1, d], near_send, near_recv.at[q - 1, d], z_one[d]).start()
        for i, dz in enumerate((6, 2, 0)):
            acc = dense(q, dz)
            for t in range(OWNED):
                dens[q - 1, i, t] = acc[t]

    def second_z(q):
        for d in BOTH:
            arrived(far_in.at[q - 1, d], far_recv.at[q - 1, d])
            arrived(near_in.at[q - 1, d], near_recv.at[q - 1, d])
            total = dens[q - 1, d] + near_in[q - 1, d, 1].astype(F32)
            far = far_in[q - 1, d].astype(F32)
            lo, hi = total[:HALF_T], total[HALF_T:]
            if d == RIGHT:
                lo = lo + far
            else:
                hi = hi + far
            mid_out[q - 1, d, :HALF_T] = lo.astype(BF16)
            mid_out[q - 1, d, HALF_T:] = hi.astype(BF16)
            remote(mid_out.at[q - 1, d], mid_in.at[q - 1, d], mid_send, mid_recv.at[q - 1, d], z_two[d]).start()

    def finish(q):
        h, cols = q // 2, slice((q % 2) * COLS, (q % 2 + 1) * COLS)
        total = dens[q - 1, 2]
        for d in BOTH:
            total = total + near_in[q - 1, d, 0].astype(F32)
        for d in BOTH:
            arrived(mid_in.at[q - 1, d], mid_recv.at[q - 1, d])
            total = total + mid_in[q - 1, d].astype(F32)
        out_ref[:, h * ROWS : (h + 1) * ROWS, cols] = total.astype(BF16)

    for cp in loads[:5]:
        cp.wait()
    for p in range(PAIRS):
        dcol[p] = jnp.full((128,), dest_s[p], I32)
        tcol[p] = jnp.full((128,), tgt_s[p], I32)
    lane = lax.broadcasted_iota(I32, (PAIRS, 128), 1)
    prow = lax.broadcasted_iota(I32, (PAIRS, 128), 0)
    same = dcol[...] == lane
    low = jnp.min(jnp.where(same, prow, PAIRS), axis=0, keepdims=True)
    high = jnp.max(jnp.where(same, prow, -1), axis=0, keepdims=True)
    low_t = jnp.max(jnp.where(same & (prow == low), tcol[...], -1), axis=0, keepdims=True)
    high_t = jnp.max(jnp.where(same & (prow == high) & (high > low), tcol[...], -1), axis=0, keepdims=True)
    tables[0] = jnp.concatenate(
        [jnp.clip(low, 0, PAIRS - 1), jnp.clip(high, 0, PAIRS - 1), low_t, high_t, jnp.zeros((4, 128), I32)], axis=0
    )
    to_smem = pltpu.make_async_copy(tables.at[0], table_s, table_sem)
    to_smem.start()
    for cp in loads[5:]:
        cp.wait()

    compute(0)
    to_smem.wait()
    pl.semaphore_wait(barrier, len(peers))
    core_copy(0, 0).start()
    core_copy(1, 0).start()
    for d in range(1, NY):
        remote(tables.at[0], tables.at[d], table_send, table_recv, at_y(d)).start()
    for d in range(1, NZ):
        remote(tables.at[0], tables_z.at[d], table_z_send, table_z_recv, at_z(d)).start()
    tables_z[0] = tables[0]

    def loop(b, _):
        compute(b)
        core_copy(0, b).start()
        core_copy(1, b).start()
        stage_x(b - 1)
        stage_a(b - 1)
        return 0

    lax.fori_loop(1, NB, loop, 0)
    stage_x(NB - 1)
    stage_a(NB - 1)
    for b in range(NB - 2):
        stage_b(b)
    send_b(0, 0, NB - 2)
    arrived(tables.at[1:], table_recv)
    arrived(tables_z.at[1:], table_z_recv)
    lane = lax.broadcasted_iota(I32, (NY, 8, 128), 2)
    for dz in range(NZ):
        mine = jnp.sum(jnp.where(lane == y_at[0] + z_at[dz], tables[...], 0), axis=2, keepdims=True)
        labels[dz] = jnp.broadcast_to(mine, (NY, 8, 128))
    lane = lax.broadcasted_iota(I32, (NZ, 8, 128), 2)
    for dy in range(NY):
        mine = jnp.sum(jnp.where(lane == y_at[dy] + z, tables_z[...], 0), axis=2, keepdims=True)
        labels_z[dy] = jnp.broadcast_to(mine, (NZ, 8, 128))
    for b in range(NB):
        stage_sum0(b)
    send_z()
    send_y(1)
    for b in range(NB - 2, NB):
        stage_b(b)
    send_b(0, NB - 2, NB)
    send_b(1, 0, NB)
    stage_sum1(0)
    send_y(2)
    first_z(1)
    stage_sum1(1)
    send_y(3)
    row_z()
    first_z(2)
    second_z(1)
    first_z(3)
    finish_z()
    second_z(2)
    finish(1)
    second_z(3)
    finish(2)
    finish(3)

    left(tables.at[1:], table_send)
    left(tables_z.at[1:], table_z_send)
    left(core_in, core_send)
    left(x_out, x_send)
    left(a_out, a_send)
    left(b_out, b_send)
    left(zslot_out, zs_send)
    left(row_out, row_send)
    left(slot_out, y_send)
    left(near_out, near_send)
    left(far_out, far_send)
    left(mid_out, mid_send)


def shards(psi, left_env, right_env, pair_source, pair_left, pair_right, pair_dest, pair_target):
    block, tile = (ROWS, WIDTH), (ROWS, COLS)
    dma = pltpu.SemaphoreType.DMA
    return pl.pallas_call(
        kernel,
        out_shape=jax.ShapeDtypeStruct((OWNED, 2 * ROWS, WIDTH), BF16),
        in_specs=[pl.BlockSpec(memory_space=pl.ANY)] * 8,
        out_specs=pl.BlockSpec(memory_space=pltpu.VMEM),
        scratch_shapes=[
            pltpu.VMEM((OWNED, WIDTH, WIDTH), BF16),
            pltpu.VMEM((4, TERMS, WIDTH, WIDTH), BF16),
            pltpu.VMEM((4, TERMS, WIDTH, WIDTH), BF16),
        ]
        + [pltpu.SMEM((PAIRS,), I32)] * 5
        + [
            pltpu.VMEM((BATCH, TERMS, WIDTH, WIDTH), BF16),
            pltpu.VMEM((2, NCORE, NB, NX, BATCH) + block, BF16),
            pltpu.VMEM((2, NB, NX, BATCH) + block, BF16),
            pltpu.VMEM((NB, NX - 1, BATCH) + block, BF16),
            pltpu.VMEM((NB, NX - 1, BATCH) + block, BF16),
            pltpu.VMEM((NB, 2, SUB) + block, BF16),
            pltpu.VMEM((NB, 2, SUB) + block, BF16),
            pltpu.VMEM((2, 2, PAIRS) + tile, BF16),
            pltpu.VMEM((2, 2, PAIRS) + tile, BF16),
            pltpu.VMEM((2, PAIRS) + block, BF16),
            pltpu.VMEM((NZ - 1, NY, CAP) + tile, BF16),
            pltpu.VMEM((NZ, NY, CAP) + tile, BF16),
            pltpu.VMEM((OWNED,) + tile, F32),
            pltpu.VMEM((NY - 1, OWNED) + tile, BF16),
            pltpu.VMEM((NY - 1, OWNED) + tile, BF16),
            pltpu.VMEM((CHUNKS - 1, NY - 1, NZ, CAP) + tile, BF16),
            pltpu.VMEM((CHUNKS - 1, NY, NZ, CAP) + tile, BF16),
            pltpu.VMEM((CHUNKS - 1, 3, OWNED) + tile, F32),
            pltpu.VMEM((CHUNKS - 1, 2, 2, OWNED) + tile, BF16),
            pltpu.VMEM((CHUNKS - 1, 2, 2, OWNED) + tile, BF16),
            pltpu.VMEM((CHUNKS - 1, 2, HALF_T) + tile, BF16),
            pltpu.VMEM((CHUNKS - 1, 2, HALF_T) + tile, BF16),
            pltpu.VMEM((CHUNKS - 1, 2, OWNED) + tile, BF16),
            pltpu.VMEM((CHUNKS - 1, 2, OWNED) + tile, BF16),
            pltpu.VMEM((PAIRS, 128), I32),
            pltpu.VMEM((PAIRS, 128), I32),
            pltpu.SMEM((8, 128), I32),
            pltpu.VMEM((NY, 8, 128), I32),
            pltpu.VMEM((NZ, 8, 128), I32),
            pltpu.VMEM((NZ, NY, 8, 128), I32),
            pltpu.VMEM((NY, NZ, 8, 128), I32),
            dma((8,)), dma, dma, dma, dma, dma,
            dma, dma((2, NB)), dma, dma((NB,)), dma, dma((NB,)), dma, dma((2,)),
            dma, dma, dma, dma, dma, dma((CHUNKS - 1,)),
            dma, dma((CHUNKS - 1, 2)), dma, dma((CHUNKS - 1, 2)), dma, dma((CHUNKS - 1, 2)),
        ],
        compiler_params=pltpu.CompilerParams(
            collective_id=0, has_side_effects=True, vmem_limit_bytes=56 * 2**20
        ),
        name="sigma",
    )(
        psi,
        left_env.reshape((4, TERMS, WIDTH, WIDTH)),
        right_env.reshape((4, TERMS, WIDTH, WIDTH)),
        pair_source, pair_left, pair_right, pair_dest.reshape(PAIRS), pair_target,
    )


def solution(mesh):
    placed = (
        P("sector", None, None),
        P("term", "sector", None, None, None),
        P("term", "sector", None, None, None),
        P("sector"),
        P("sector"),
        P("sector"),
        P("sector", None),
        P("sector"),
    )
    return jax.shard_map(
        shards, mesh=mesh, in_specs=placed, out_specs=P("sector", "term", None), check_vma=False
    )
```

time: 56.7 us -> 52 us (0.917)
  the two profiles are of different devices: /device:TPU:1 before, /device:TPU:2 now
where the time goes in v4:
time: 52 us; the launch traced here: 51.9 us
  Pallas kernels  50.3 us (97%)
  local copies, waits for them, and re-layouts  1.57 us (3%)
    pallas_call x1, Pallas kernels, shards(): pl.pallas_call(kernel, out_shape=jax.ShapeDtypeStruct((OWNED, 2 * ROWS, W...  50.3 us
    unnamed x1, local copies, waits for them, and re-layouts  1.57 us

profile of v4, /device:TPU:2, one launch (start us, length us, event | category | flops | bytes accessed | tf_op | source)
XLA Modules:
  0.0 51.9 jit_solution(10622454989486138448)
XLA Ops:
  0.0 50.3 %sigma.1 = bf16[8,32,256]{2,1,0:T(8,128)(2,1)} custom-call(bf16[8,256,256]{2,1,0:T(8,128)(2,1)} %psi_hbm.1, bf16[4,4,256,256]{3,2,1,0:T(8,128)(2,1)} %bitcast.3, bf16[4,4,256,256]{3,2,1,0:T(8,128)(2,1)} %bitcast.4, s32[32]{0:T(128)} %src_hbm.1, s32[32]{0:T(128)} %lft_hbm.1, s32[32]{0:T(128)} %rgt_hbm.1, s32[32]{0:T(128)} %bitcast.5, s32[32]{0:T(128)} %tgt_hbm.1), custom_call_target="tpu_custom_call" | custom-call | tf_op jit(solution)/shard_map/sigma/pallas_call | solution.py:356
  50.3 1.6 %copy.10 = bf16[8,32,256]{2,1,0:T(8,128)(2,1)} copy(bf16[8,32,256]{2,1,0:T(8,128)(2,1)} %sigma.1) | data formatting | bytes 262144

commit v5 on v4

--- a/solution.py
+++ b/solution.py
@@ -157,40 +157,47 @@
             term_ = jnp.where(lab == t, blk, 0.0)
             acc[t] = term_ if acc[t] is None else acc[t] + term_
 
-    def send_z():
+    def send_z(q):
+        h, i, cols = q // 2, q, slice((q % 2) * COLS, (q % 2 + 1) * COLS)
         for dz in (4, 3, 5, 2, 6, 1, 7, 0):
             for dy in range(NY):
                 o = y_at[dy] + z_at[dz]
                 for s in range(CAP):
-                    blk = red[0, table_s[s, o], :, :COLS]
+                    blk = red[h, table_s[s, o], :, cols]
                     if dz:
-                        zslot_out[dz - 1, dy, s] = blk
+                        zslot_out[i, dz - 1, dy, s] = blk
                     else:
-                        zslot_in[0, dy, s] = blk
+                        zslot_in[i, 0, dy, s] = blk
             if dz:
-                remote(zslot_out.at[dz - 1], zslot_in.at[dz], zs_send, zs_recv, at_z(dz)).start()
-
-    def row_z():
-        arrived(zslot_in.at[1:], zs_recv)
+                remote(
+                    zslot_out.at[i, dz - 1], zslot_in.at[i, dz], zs_send.at[i], zs_recv.at[i], at_z(dz)
+                ).start()
+
+    def row_z(q):
+        i = q
+        arrived(zslot_in.at[i, 1:], zs_recv.at[i])
         for dy in (2, 1, 3, 0):
             acc = [None] * OWNED
             for dz in range(NZ):
                 for s in range(CAP):
-                    add_slot(acc, zslot_in[dz, dy, s], labels_z[dy, dz, 2 + s : 3 + s, :])
+                    add_slot(acc, zslot_in[i, dz, dy, s], labels_z[dy, dz, 2 + s : 3 + s, :])
             for t in range(OWNED):
                 if dy:
-                    row_out[dy - 1, t] = acc[t].astype(BF16)
+                    row_out[i, dy - 1, t] = acc[t].astype(BF16)
                 else:
-                    own[t] = acc[t]
+                    own[i, t] = acc[t]
             if dy:
-                remote(row_out.at[dy - 1], row_in.at[dy - 1], row_send, row_recv, at_y(dy)).start()
-
-    def finish_z():
-        arrived(row_in, row_recv)
-        total = own[...]
+                remote(
+                    row_out.at[i, dy - 1], row_in.at[i, dy - 1], row_send.at[i], row_recv.at[i], at_y(dy)
+                ).start()
+
+    def finish_z(q):
+        h, i, cols = q // 2, q, slice((q % 2) * COLS, (q % 2 + 1) * COLS)
+        arrived(row_in.at[i], row_recv.at[i])
+        total = own[i]
         for dy in range(1, NY):
-            total = total + row_in[dy - 1].astype(F32)
-        out_ref[:, :ROWS, :COLS] = total.astype(BF16)
+            total = total + row_in[i, dy - 1].astype(F32)
+        out_ref[:, h * ROWS : (h + 1) * ROWS, cols] = total.astype(BF16)
 
     def send_y(q):
         h, cols = q // 2, slice((q % 2) * COLS, (q % 2 + 1) * COLS)
@@ -200,61 +207,61 @@
                 for s in range(CAP):
                     blk = red[h, table_s[s, o], :, cols]
                     if dy:
-                        slot_out[q - 1, dy - 1, dz, s] = blk
+                        slot_out[q - 2, dy - 1, dz, s] = blk
                     else:
-                        slot_in[q - 1, 0, dz, s] = blk
+                        slot_in[q - 2, 0, dz, s] = blk
             if dy:
-                remote(slot_out.at[q - 1, dy - 1], slot_in.at[q - 1, dy], y_send, y_recv.at[q - 1], at_y(dy)).start()
+                remote(slot_out.at[q - 2, dy - 1], slot_in.at[q - 2, dy], y_send, y_recv.at[q - 2], at_y(dy)).start()
 
     def dense(q, dz):
         acc = [None] * OWNED
         for dy in range(NY):
             for s in range(CAP):
-                add_slot(acc, slot_in[q - 1, dy, dz, s], labels[dz, dy, 2 + s : 3 + s, :])
+                add_slot(acc, slot_in[q - 2, dy, dz, s], labels[dz, dy, 2 + s : 3 + s, :])
         return acc
 
     def first_z(q):
-        arrived(slot_in.at[q - 1, 1:], y_recv.at[q - 1])
+        arrived(slot_in.at[q - 2, 1:], y_recv.at[q - 2])
         acc = dense(q, 4)
         for t in range(HALF_T):
-            far_out[q - 1, RIGHT, t] = acc[t].astype(BF16)
-            far_out[q - 1, LEFT, t] = acc[HALF_T + t].astype(BF16)
-        for d in BOTH:
-            remote(far_out.at[q - 1, d], far_in.at[q - 1, d], far_send, far_recv.at[q - 1, d], z_two[d]).start()
+            far_out[q - 2, RIGHT, t] = acc[t].astype(BF16)
+            far_out[q - 2, LEFT, t] = acc[HALF_T + t].astype(BF16)
+        for d in BOTH:
+            remote(far_out.at[q - 2, d], far_in.at[q - 2, d], far_send, far_recv.at[q - 2, d], z_two[d]).start()
         for d in BOTH:
             for i, dz in enumerate((1, 3) if d == RIGHT else (7, 5)):
                 acc = dense(q, dz)
                 for t in range(OWNED):
-                    near_out[q - 1, d, i, t] = acc[t].astype(BF16)
-            remote(near_out.at[q - 1, d], near_in.at[q - 1, d], near_send, near_recv.at[q - 1, d], z_one[d]).start()
+                    near_out[q - 2, d, i, t] = acc[t].astype(BF16)
+            remote(near_out.at[q - 2, d], near_in.at[q - 2, d], near_send, near_recv.at[q - 2, d], z_one[d]).start()
         for i, dz in enumerate((6, 2, 0)):
             acc = dense(q, dz)
             for t in range(OWNED):
-                dens[q - 1, i, t] = acc[t]
+                dens[q - 2, i, t] = acc[t]
 
     def second_z(q):
         for d in BOTH:
-            arrived(far_in.at[q - 1, d], far_recv.at[q - 1, d])
-            arrived(near_in.at[q - 1, d], near_recv.at[q - 1, d])
-            total = dens[q - 1, d] + near_in[q - 1, d, 1].astype(F32)
-            far = far_in[q - 1, d].astype(F32)
+            arrived(far_in.at[q - 2, d], far_recv.at[q - 2, d])
+            arrived(near_in.at[q - 2, d], near_recv.at[q - 2, d])
+            total = dens[q - 2, d] + near_in[q - 2, d, 1].astype(F32)
+            far = far_in[q - 2, d].astype(F32)
             lo, hi = total[:HALF_T], total[HALF_T:]
             if d == RIGHT:
                 lo = lo + far
             else:
                 hi = hi + far
-            mid_out[q - 1, d, :HALF_T] = lo.astype(BF16)
-            mid_out[q - 1, d, HALF_T:] = hi.astype(BF16)
-            remote(mid_out.at[q - 1, d], mid_in.at[q - 1, d], mid_send, mid_recv.at[q - 1, d], z_two[d]).start()
+            mid_out[q - 2, d, :HALF_T] = lo.astype(BF16)
+            mid_out[q - 2, d, HALF_T:] = hi.astype(BF16)
+            remote(mid_out.at[q - 2, d], mid_in.at[q - 2, d], mid_send, mid_recv.at[q - 2, d], z_two[d]).start()
 
     def finish(q):
         h, cols = q // 2, slice((q % 2) * COLS, (q % 2 + 1) * COLS)
-        total = dens[q - 1, 2]
-        for d in BOTH:
-            total = total + near_in[q - 1, d, 0].astype(F32)
-        for d in BOTH:
-            arrived(mid_in.at[q - 1, d], mid_recv.at[q - 1, d])
-            total = total + mid_in[q - 1, d].astype(F32)
+        total = dens[q - 2, 2]
+        for d in BOTH:
+            total = total + near_in[q - 2, d, 0].astype(F32)
+        for d in BOTH:
+            arrived(mid_in.at[q - 2, d], mid_recv.at[q - 2, d])
+            total = total + mid_in[q - 2, d].astype(F32)
         out_ref[:, h * ROWS : (h + 1) * ROWS, cols] = total.astype(BF16)
 
     for cp in loads[:5]:
@@ -282,11 +289,12 @@
     pl.semaphore_wait(barrier, len(peers))
     core_copy(0, 0).start()
     core_copy(1, 0).start()
-    for d in range(1, NY):
-        remote(tables.at[0], tables.at[d], table_send, table_recv, at_y(d)).start()
-    for d in range(1, NZ):
-        remote(tables.at[0], tables_z.at[d], table_z_send, table_z_recv, at_z(d)).start()
-    tables_z[0] = tables[0]
+    def send_tables():
+        for d in range(1, NY):
+            remote(tables.at[0], tables.at[d], table_send, table_recv, at_y(d)).start()
+        for d in range(1, NZ):
+            remote(tables.at[0], tables_z.at[d], table_z_send, table_z_recv, at_z(d)).start()
+        tables_z[0] = tables[0]
 
     def loop(b, _):
         compute(b)
@@ -294,6 +302,11 @@
         core_copy(1, b).start()
         stage_x(b - 1)
         stage_a(b - 1)
+
+        @pl.when(b == 2)
+        def _():
+            send_tables()
+
         return 0
 
     lax.fori_loop(1, NB, loop, 0)
@@ -314,25 +327,24 @@
         labels_z[dy] = jnp.broadcast_to(mine, (NZ, 8, 128))
     for b in range(NB):
         stage_sum0(b)
-    send_z()
-    send_y(1)
+    send_z(0)
+    send_z(1)
     for b in range(NB - 2, NB):
         stage_b(b)
     send_b(0, NB - 2, NB)
     send_b(1, 0, NB)
     stage_sum1(0)
     send_y(2)
-    first_z(1)
     stage_sum1(1)
     send_y(3)
-    row_z()
+    row_z(0)
     first_z(2)
-    second_z(1)
     first_z(3)
-    finish_z()
+    row_z(1)
     second_z(2)
-    finish(1)
+    finish_z(0)
     second_z(3)
+    finish_z(1)
     finish(2)
     finish(3)
 
@@ -342,8 +354,9 @@
     left(x_out, x_send)
     left(a_out, a_send)
     left(b_out, b_send)
-    left(zslot_out, zs_send)
-    left(row_out, row_send)
+    for i in range(2):
+        left(zslot_out.at[i], zs_send.at[i])
+        left(row_out.at[i], row_send.at[i])
     left(slot_out, y_send)
     left(near_out, near_send)
     left(far_out, far_send)
@@ -375,20 +388,20 @@
             pltpu.VMEM((2, 2, PAIRS) + tile, BF16),
             pltpu.VMEM((2, 2, PAIRS) + tile, BF16),
             pltpu.VMEM((2, PAIRS) + block, BF16),
-            pltpu.VMEM((NZ - 1, NY, CAP) + tile, BF16),
-            pltpu.VMEM((NZ, NY, CAP) + tile, BF16),
-            pltpu.VMEM((OWNED,) + tile, F32),
-            pltpu.VMEM((NY - 1, OWNED) + tile, BF16),
-            pltpu.VMEM((NY - 1, OWNED) + tile, BF16),
-            pltpu.VMEM((CHUNKS - 1, NY - 1, NZ, CAP) + tile, BF16),
-            pltpu.VMEM((CHUNKS - 1, NY, NZ, CAP) + tile, BF16),
-            pltpu.VMEM((CHUNKS - 1, 3, OWNED) + tile, F32),
-            pltpu.VMEM((CHUNKS - 1, 2, 2, OWNED) + tile, BF16),
-            pltpu.VMEM((CHUNKS - 1, 2, 2, OWNED) + tile, BF16),
-            pltpu.VMEM((CHUNKS - 1, 2, HALF_T) + tile, BF16),
-            pltpu.VMEM((CHUNKS - 1, 2, HALF_T) + tile, BF16),
-            pltpu.VMEM((CHUNKS - 1, 2, OWNED) + tile, BF16),
-            pltpu.VMEM((CHUNKS - 1, 2, OWNED) + tile, BF16),
+            pltpu.VMEM((2, NZ - 1, NY, CAP) + tile, BF16),
+            pltpu.VMEM((2, NZ, NY, CAP) + tile, BF16),
+            pltpu.VMEM((2, OWNED) + tile, F32),
+            pltpu.VMEM((2, NY - 1, OWNED) + tile, BF16),
+            pltpu.VMEM((2, NY - 1, OWNED) + tile, BF16),
+            pltpu.VMEM((CHUNKS - 2, NY - 1, NZ, CAP) + tile, BF16),
+            pltpu.VMEM((CHUNKS - 2, NY, NZ, CAP) + tile, BF16),
+            pltpu.VMEM((CHUNKS - 2, 3, OWNED) + tile, F32),
+            pltpu.VMEM((CHUNKS - 2, 2, 2, OWNED) + tile, BF16),
+            pltpu.VMEM((CHUNKS - 2, 2, 2, OWNED) + tile, BF16),
+            pltpu.VMEM((CHUNKS - 2, 2, HALF_T) + tile, BF16),
+            pltpu.VMEM((CHUNKS - 2, 2, HALF_T) + tile, BF16),
+            pltpu.VMEM((CHUNKS - 2, 2, OWNED) + tile, BF16),
+            pltpu.VMEM((CHUNKS - 2, 2, OWNED) + tile, BF16),
             pltpu.VMEM((PAIRS, 128), I32),
             pltpu.VMEM((PAIRS, 128), I32),
             pltpu.SMEM((8, 128), I32),
@@ -398,8 +411,8 @@
             pltpu.VMEM((NY, NZ, 8, 128), I32),
             dma((8,)), dma, dma, dma, dma, dma,
             dma, dma((2, NB)), dma, dma((NB,)), dma, dma((NB,)), dma, dma((2,)),
-            dma, dma, dma, dma, dma, dma((CHUNKS - 1,)),
-            dma, dma((CHUNKS - 1, 2)), dma, dma((CHUNKS - 1, 2)), dma, dma((CHUNKS - 1, 2)),
+            dma((2,)), dma((2,)), dma((2,)), dma((2,)), dma, dma((CHUNKS - 2,)),
+            dma, dma((CHUNKS - 2, 2)), dma, dma((CHUNKS - 2, 2)), dma, dma((CHUNKS - 2, 2)),
         ],
         compiler_params=pltpu.CompilerParams(
             collective_id=0, has_side_effects=True, vmem_limit_bytes=56 * 2**20

time: 52 us -> 51.5 us (level)
  Pallas kernels: 50.3 us -> 49.4 us
    pallas_call x1, Pallas kernels: 50.3 us -> 49.4 us  [shards(): pl.pallas_call(kernel, out_shape=jax.ShapeDtypeStruct((OWNED, 2 * ROWS, W...]
where the time goes in v5:
time: 51.5 us; the launch traced here: 51 us
  Pallas kernels  49.4 us (96%)
  local copies, waits for them, and re-layouts  1.57 us (3%)
    pallas_call x1, Pallas kernels, shards(): pl.pallas_call(kernel, out_shape=jax.ShapeDtypeStruct((OWNED, 2 * ROWS, W...  49.4 us
    unnamed x1, local copies, waits for them, and re-layouts  1.57 us

profile of v5, /device:TPU:2, one launch (start us, length us, event | category | flops | bytes accessed | tf_op | source)
XLA Modules:
  0.0 51.0 jit_solution(4491638690355029025)
XLA Ops:
  0.0 49.4 %sigma.1 = bf16[8,32,256]{2,1,0:T(8,128)(2,1)} custom-call(bf16[8,256,256]{2,1,0:T(8,128)(2,1)} %psi_hbm.1, bf16[4,4,256,256]{3,2,1,0:T(8,128)(2,1)} %bitcast.3, bf16[4,4,256,256]{3,2,1,0:T(8,128)(2,1)} %bitcast.4, s32[32]{0:T(128)} %src_hbm.1, s32[32]{0:T(128)} %lft_hbm.1, s32[32]{0:T(128)} %rgt_hbm.1, s32[32]{0:T(128)} %bitcast.5, s32[32]{0:T(128)} %tgt_hbm.1), custom_call_target="tpu_custom_call" | custom-call | tf_op jit(solution)/shard_map/sigma/pallas_call | solution.py:369
  49.4 1.6 %copy.10 = bf16[8,32,256]{2,1,0:T(8,128)(2,1)} copy(bf16[8,32,256]{2,1,0:T(8,128)(2,1)} %sigma.1) | data formatting | bytes 262144

commit v6 on v5

--- a/solution.py
+++ b/solution.py
@@ -55,7 +55,7 @@
     small = [(src_hbm, src_s), (lft_hbm, lft_s), (rgt_hbm, rgt_s), (dest_hbm, dest_s), (tgt_hbm, tgt_s)]
     loads = small + [(psi_hbm, psi), (right_hbm, renv), (left_hbm, lenv)]
     loads = [pltpu.make_async_copy(a, b, load_sem.at[i]) for i, (a, b) in enumerate(loads)]
-    for cp in loads:
+    for cp in loads[5:] + loads[:5]:
         cp.start()
 
     barrier = pltpu.get_barrier_semaphore()

time: 51.5 us -> 51.5 us (level)
  no operation moved by 1% of the time
where the time goes in v6:
time: 51.5 us; the launch traced here: 51 us
  Pallas kernels  49.4 us (96%)
  local copies, waits for them, and re-layouts  1.57 us (3%)
    pallas_call x1, Pallas kernels, shards(): pl.pallas_call(kernel, out_shape=jax.ShapeDtypeStruct((OWNED, 2 * ROWS, W...  49.4 us
    unnamed x1, local copies, waits for them, and re-layouts  1.57 us

profile of v6, /device:TPU:2, one launch (start us, length us, event | category | flops | bytes accessed | tf_op | source)
XLA Modules:
  0.0 51.0 jit_solution(4872990311162583951)
XLA Ops:
  0.0 49.4 %sigma.1 = bf16[8,32,256]{2,1,0:T(8,128)(2,1)} custom-call(bf16[8,256,256]{2,1,0:T(8,128)(2,1)} %psi_hbm.1, bf16[4,4,256,256]{3,2,1,0:T(8,128)(2,1)} %bitcast.3, bf16[4,4,256,256]{3,2,1,0:T(8,128)(2,1)} %bitcast.4, s32[32]{0:T(128)} %src_hbm.1, s32[32]{0:T(128)} %lft_hbm.1, s32[32]{0:T(128)} %rgt_hbm.1, s32[32]{0:T(128)} %bitcast.5, s32[32]{0:T(128)} %tgt_hbm.1), custom_call_target="tpu_custom_call" | custom-call | tf_op jit(solution)/shard_map/sigma/pallas_call | solution.py:369
  49.4 1.6 %copy.10 = bf16[8,32,256]{2,1,0:T(8,128)(2,1)} copy(bf16[8,32,256]{2,1,0:T(8,128)(2,1)} %sigma.1) | data formatting | bytes 262144
